TPU v7x, 256 devices: a whole 4x4x8 slice. The times are simulated.
256 devices in a mesh: row: 16 (over z, y_lo), col: 16 (over y_hi, x, core).
Axes of the slice: x: 4, y: 4 (y_hi: 2, y_lo: 2; y = y_hi * 2 + y_lo), z: 8, core: 2. Of those that a mesh axis runs over, the one named last changes fastest.
Arguments:
- matrix: float32 [2, 8192, 2, 8192], P(None, 'row', None, 'col'), may hold values from -6 to 6
- pivot_rows: int32 [512], replicated, may hold values from 0 to 16383, as said below
- inv_lower: float32 [512, 512], replicated, as said below
- inv_upper: float32 [512, 512], replicated, as said below
Outputs:
- factored: float32 [2, 8192, 2, 8192], P(None, 'row', None, 'col')
Inputs may be any that keep to these rules, and one draw needn't show every extreme that they name: Each pivot_rows[i] is either i or a row of 512 or more; no row appears twice. inv_lower is unit lower triangular. inv_upper is upper triangular with a positive diagonal.
All inputs are finite; a program needn't handle non-finite values.
Results may differ from a plain program's by a relative error of at most 0.00008.
Values sent between devices are 32-bit elements; how exact they have to be, the bound alone decides.
No kernel may reach another device: no remote copies, remote signals or barrier semaphores. Data moves between devices by JAX's collectives and lax.ppermute only.
A program may use at most 64 MiB of HBM per device.

v0:
```python
import jax
import jax.numpy as jnp
from jax import lax
from jax.sharding import PartitionSpec as P


def spread(block, axis, holder):
    block = jnp.where(lax.axis_index(axis) == holder, block, jnp.zeros_like(block))
    return lax.psum(block, axis)


def local(matrix, pivot_rows, inv_lower, inv_upper):
    best = lax.Precision.HIGHEST
    tiles_down, tile_width, tiles_across, _ = matrix.shape
    row_count = lax.axis_size("row")
    row_index = lax.axis_index("row")
    col_index = lax.axis_index("col")
    local_rows = tiles_down * tile_width
    matrix_here = matrix.reshape(local_rows, tiles_across * tile_width)
    positions = jnp.arange(local_rows, dtype=jnp.int32)
    global_rows = (
        positions // tile_width * row_count + row_index
    ) * tile_width + positions % tile_width
    pivot_tile = pivot_rows // tile_width
    owned = pivot_tile % row_count == row_index
    pivot_local = pivot_tile // row_count * tile_width + pivot_rows % tile_width
    picked = jnp.where(
        owned[:, None], matrix_here[jnp.where(owned, pivot_local, 0)], jnp.float32(0.0)
    )
    former_top = spread(matrix_here[:tile_width], "row", 0)
    matches = (global_rows[:, None] == pivot_rows[None, :]) & (global_rows[:, None] >= tile_width)
    has_source = jnp.any(matches, axis=1)
    source = jnp.sum(
        jnp.where(matches, jnp.arange(tile_width, dtype=jnp.int32)[None, :], 0), axis=1
    )
    swapped = jnp.where(has_source[:, None], former_top[source], matrix_here)
    new_top = lax.psum(picked, "row")
    upper_rows = jnp.dot(inv_lower, new_top, precision=best, preferred_element_type=jnp.float32)
    panel_rows = swapped[:, :tile_width]
    solved_panel = jnp.dot(
        panel_rows, inv_upper, precision=best, preferred_element_type=jnp.float32
    )
    lower_cols = spread(solved_panel, "col", 0)
    updated = swapped - jnp.dot(
        lower_cols, upper_rows, precision=best, preferred_element_type=jnp.float32
    )
    leading = jnp.where(col_index == 0, lower_cols, updated[:, :tile_width])
    result = jnp.concatenate([leading, updated[:, tile_width:]], axis=1)
    first_rows = jnp.where(row_index == 0, upper_rows, result[:tile_width])
    result = jnp.concatenate([first_rows, result[tile_width:]], axis=0)
    return result.reshape(tiles_down, tile_width, tiles_across, tile_width)


def solution(mesh):
    return jax.shard_map(
        local,
        mesh=mesh,
        in_specs=(P(None, "row", None, "col"), P(), P(), P()),
        out_specs=P(None, "row", None, "col"),
        check_vma=False,
    )
```

profile of v0, /device:TPU:58, one launch (start us, length us, event | category | flops | bytes accessed | tf_op | source)
XLA Modules:
  0.0 414.7 jit_solution(5607492961678541795)
XLA Ops:
  6.5 0.8 compare_select_fusion.1
  7.3 2.5 slice_select_fusion.1
  9.9 1.8 copy.10
  11.7 1.1 copy-done.2
  12.8 3.0 copy.9
  15.8 5.0 %gather_fusion = f32[512,1024]{1,0:T(8,128)S(1)} fusion(f32[1024,1024]{1,0:T(8,128)} %bitcast.15, s32[1024]{0:T(1024)S(1)} %pad_clamp_fusion), kind=kCustom, calls=%fused_computation | custom fusion | bytes 4196352 | tf_op jit(solution)/shard_map/gather | solution.py:28
  20.8 1.5 broadcast_select_fusion.1
  22.3 0.0 all-reduce.6.cloned.1.call-update
  22.4 0.2 all-reduce.4.cloned.1.call-start
  22.6 0.4 copy-done.4
  23.0 0.9 fusion.6
  23.9 1.0 select_reduce_fusion
  25.0 199.8 %all-reduce.6.cloned.1.call-done = (f32[512,1024]{1,0:T(8,128)}, f32[512,1024]{1,0:T(8,128)}) async-done(((f32[512,1024]{1,0:T(8,128)}, f32[512,1024]{1,0:T(8,128)}), (f32[512,1024]{1,0:T(8,128)}, f32[512,1024]{1,0:T(8,128)})) %all-reduce.6.cloned.1.call-update) | async-done | bytes 4194320 | tf_op jit(solution)/shard_map/psum | solution.py:9
  224.8 7.9 %gather_fusion.1 = f32[1024,1024]{1,0:T(8,128)} fusion(f32[512,1024]{1,0:T(8,128)} %get-tuple-element.5, s32[1024]{0:T(1024)S(1)} %broadcast_clamp_fusion), kind=kCustom, calls=%fused_computation.1 | custom fusion | bytes 8392704 | tf_op jit(solution)/shard_map/gather | solution.py:36
  232.7 3.9 broadcast_select_fusion
  236.7 2.0 copy-done.1
  238.7 4.8 %fusion.7 = f32[1024,512]{1,0:T(8,128)} fusion(f32[512,512]{1,0:T(8,128)S(1)} %copy-done, f32[1024,1024]{1,0:T(8,128)S(1)} %broadcast_select_fusion, pred[]{:T(512)S(6)} %eq.35), kind=kOutput, calls=%fused_computation.20 | convolution fusion | flops 3221749760 | bytes 5242881 | tf_op jit(solution)/shard_map/dot_general | solution.py:40
  243.5 5.4 %fusion.29 = f32[1024,512]{0,1:T(8,128)S(1)} fusion(f32[512,1024]{1,0:T(8,128)} %get-tuple-element.6, f32[512,512]{1,0:T(8,128)} %param.6), kind=kOutput, calls=%fused_computation.63 | convolution fusion | flops 3221225472 | bytes 5242880 | tf_op jit(solution)/shard_map/dot_general | solution.py:38
  248.9 139.5 %all-reduce.4.cloned.1.call-done = f32[1024,512]{1,0:T(8,128)} async-done(((f32[1024,512]{1,0:T(8,128)}), f32[1024,512]{1,0:T(8,128)}) %all-reduce.4.cloned.1.call-update) | async-done | bytes 2097168 | tf_op jit(solution)/shard_map/psum | solution.py:9
  388.3 9.5 %convolution_subtract_fusion = f32[1024,1024]{1,0:T(8,128)S(1)} fusion(f32[1024,1024]{1,0:T(8,128)} %copy-done.1, f32[1024,512]{1,0:T(8,128)} %all-reduce.4.cloned.1.call-done, f32[1024,512]{0,1:T(8,128)S(1)} %fusion.29), kind=kOutput, calls=%fused_computation.9 | convolution fusion | flops 6443499520 | bytes 12582912 | tf_op jit(solution)/shard_map/dot_general | solution.py:44
  397.9 0.7 fusion.28
  398.6 0.4 fusion.3
  399.0 2.3 fusion.1
  401.3 6.6 %reshape.55 = f32[2,512,2,512]{3,2,1,0:T(2,128)} reshape(f32[1024,1024]{1,0:T(8,128)} %fusion.1) | data formatting | bytes 8388608 | tf_op jit(solution)/shard_map/reshape | solution.py:51
  (14 shorter events, 0.1 us)
Async XLA Ops:
  6.5 232.2 %copy-start = (f32[512,512]{1,0:T(8,128)S(1)}, f32[512,512]{1,0:T(8,128)}, u32[]{:S(2)}) copy-start(f32[512,512]{1,0:T(8,128)} %param.7) | copy-start | bytes 3145732
  6.5 218.3 %all-reduce.6.cloned.1.call-start = ((), (), s32[]{:S(2)}) async-start(), calls=%async_computation.1 | async-start | bytes 8388608 | tf_op jit(solution)/shard_map/psum | solution.py:9
  9.8 2.9 copy-start.2
  22.3 0.7 copy-start.4
  22.4 366.0 %all-reduce.4.cloned.1.call-start = ((), (), s32[]{:S(2)}) async-start(), calls=%async_computation | async-start | bytes 4194304 | tf_op jit(solution)/shard_map/psum | solution.py:9
  236.7 2.0 copy-start.1
  388.3 9.5 %copy-start.3 = (f32[1024,512]{1,0:T(8,128)S(1)}, f32[1024,512]{1,0:T(8,128)}, u32[]{:S(2)}) copy-start(f32[1024,512]{1,0:T(8,128)} %all-reduce.4.cloned.1.call-done) | copy-start | bytes 6291460
Sparse Core Ops, SparseCore 0:
  22.5 202.2 all-reduce.5
  243.6 144.6 all-reduce.3
where the time goes:
time: 421 us; the launch traced here: 415 us
  waiting for transfers between devices  339 us (81%)
  local copies, waits for them, and re-layouts  27.9 us (7%)
  matrix products  19.6 us (5%)
  other arithmetic  14.1 us (3%)
  between operations  13.5 us (3%)
    psum x2, waiting for transfers between devices, spread(): return lax.psum(block, axis)  339 us
    dot_general x1, matrix products, local(): jnp.dot(lower_cols, upper_rows, precision=best, preferred_element_type=jn...  9.52 us
  transfers between devices with their start and end apart: 2, of which 2 were waited for; matrix products, arithmetic and copies ran while one was open for 2% of the time, Pallas kernels for 0%

commit v1 on v0

--- a/solution.py
+++ b/solution.py
@@ -1,7 +1,18 @@
+import functools
+
 import jax
 import jax.numpy as jnp
 from jax import lax
+from jax.experimental import pallas as pl
+from jax.experimental.pallas import tpu as pltpu
 from jax.sharding import PartitionSpec as P
+
+CAP = 48
+TILE = 512
+LAYERS = 8
+MIB = 1024 * 1024
+VMEM = 60 * MIB
+FAR, NEAR = (4, 3, 5, 2), (6, 1, 7, 0)
 
 
 def spread(block, axis, holder):
@@ -9,7 +20,7 @@
     return lax.psum(block, axis)
 
 
-def local(matrix, pivot_rows, inv_lower, inv_upper):
+def any_pivots(matrix, pivot_rows, inv_lower, inv_upper):
     best = lax.Precision.HIGHEST
     tiles_down, tile_width, tiles_across, _ = matrix.shape
     row_count = lax.axis_size("row")
@@ -51,6 +62,383 @@
     return result.reshape(tiles_down, tile_width, tiles_across, tile_width)
 
 
+def as_rows(matrix):
+    return matrix.reshape(1024, 2, 4, 128).transpose(0, 2, 1, 3).reshape(1024, 8, 128)
+
+
+def as_matrix(rows):
+    return rows.reshape(1024, 4, 2, 128).transpose(0, 2, 1, 3).reshape(2, 512, 2, 512)
+
+
+def split(value):
+    high = value.astype(jnp.bfloat16)
+    low = (value - high.astype(jnp.float32)).astype(jnp.bfloat16)
+    return high, low
+
+
+def dot3(a_high, a_low, b_high, b_low):
+    dot = functools.partial(jnp.dot, preferred_element_type=jnp.float32)
+    return dot(a_high, b_high) + (dot(a_high, b_low) + dot(a_low, b_high))
+
+
+def whole(memory, count):
+    return [pl.BlockSpec(memory_space=memory)] * count
+
+
+def prepare_kernel(rows_ref, key_ref, x_ref, first_ref, second_ref, picked_ref, *rest):
+    outs, (x_here, load) = rest[: LAYERS + 2], rest[LAYERS + 2 :]
+    loads = [
+        pltpu.make_async_copy(x_ref.at[pl.ds(2048 * b, 2048)], x_here.at[pl.ds(2048 * b, 2048)], load.at[b])
+        for b in range(4)
+    ]
+    for copy in loads:
+        copy.start()
+    places = [(outs[k // 2], 0) for k in range(16)]
+    for group, out in zip((FAR, NEAR), outs[LAYERS:]):
+        for at, k in enumerate(group):
+            places[2 * k + 1] = (out, 320 * at)
+    for b in range(4):
+        loads[b].wait()
+        out_ref = (first_ref, second_ref)[b // 2]
+        for l in range(4):
+            out_ref[256 * (b % 2) : 256 * (b % 2) + 256, 128 * l : 128 * l + 128] = x_here[
+                pl.ds(2048 * b + 2 * l, 256, stride=8), :
+            ]
+        for k, (out, at) in enumerate(places):
+            if k // 8 == b:
+                out[at : at + 256, :] = x_here[256 * k : 256 * (k + 1), :]
+                out[at + 256 : at + 320, :] = jnp.zeros((64, 128), jnp.float32)
+
+    @pl.loop(0, CAP)
+    def _(k):
+        picked_ref[pl.ds(pl.multiple_of(k * 8, 8), 8), :] = x_here[
+            pl.ds(pl.multiple_of(rows_ref[8 + k] * 8, 8), 8), :
+        ]
+
+    @pl.when(rows_ref[2] == 0)
+    def _():
+        tile = first_ref[...]
+        high = tile.astype(jnp.bfloat16)
+        rest_of = tile - high.astype(jnp.float32)
+        middle = rest_of.astype(jnp.bfloat16)
+        low = (rest_of - middle.astype(jnp.float32)).astype(jnp.bfloat16)
+        for part in range(4):
+            slot = lax.broadcasted_iota(jnp.int32, (4 * CAP, TILE), 0) + 4 * CAP * part
+            choose = jnp.where(slot == key_ref[...], 1.0, 0.0).astype(jnp.bfloat16)
+            dot = functools.partial(jnp.dot, choose, preferred_element_type=jnp.float32)
+            table = dot(high) + (dot(middle) + dot(low))
+            for k in range(4):
+                out, at = places[4 * part + k]
+                for l in range(4):
+                    cols = slice(128 * l, 128 * l + 128)
+                    out[pl.ds(at + 2 * l, 40, stride=8), :] = table[CAP * k : CAP * k + 40, cols]
+                    out[pl.ds(at + 256 + 2 * l + 1, 8, stride=8), :] = table[CAP * k + 40 : CAP * k + 48, cols]
+
+
+def prepare(rows, key, x):
+    half = jax.ShapeDtypeStruct((512, 512), jnp.float32)
+    picked = jax.ShapeDtypeStruct((CAP * 8, 128), jnp.float32)
+    piece = jax.ShapeDtypeStruct((320, 128), jnp.float32)
+    group = jax.ShapeDtypeStruct((1280, 128), jnp.float32)
+    return pl.pallas_call(
+        prepare_kernel,
+        out_shape=[half, half, picked] + [piece] * LAYERS + [group] * 2,
+        in_specs=whole(pltpu.SMEM, 1) + whole(pltpu.VMEM, 1) + whole(pl.ANY, 1),
+        out_specs=whole(pltpu.VMEM, LAYERS + 5),
+        scratch_shapes=[pltpu.VMEM((8192, 128), jnp.float32), pltpu.SemaphoreType.DMA((4,))],
+        compiler_params=pltpu.CompilerParams(vmem_limit_bytes=VMEM),
+        cost_estimate=pl.CostEstimate(flops=2 * 10**9, bytes_accessed=10 * MIB, transcendentals=0),
+        name="prepare",
+    )(rows, key, x)
+
+
+def spread_rows(ref, g_high, g_low):
+    count = ref.shape[0] // 8
+    for sub in range(8):
+        high, low = split(ref[pl.ds(sub, count, stride=8), :])
+        g_high[:, 128 * sub : 128 * sub + 128] = high
+        g_low[:, 128 * sub : 128 * sub + 128] = low
+
+
+def early_kernel(
+    rows_ref, half_ref, other_ref, inv_ref, pivots_ref, take_ref, keep_ref, x_ref,
+    m_ref, lw_high, lw_low, part_high, part_low, panel, l_high, l_low, g_high, g_low, u_ref, load,
+):
+    copy = pltpu.make_async_copy(x_ref, m_ref, load)
+    copy.start()
+    core, x = rows_ref[2] % 2, rows_ref[2] // 2 % 4
+    for ref, tile in ((half_ref, core), (other_ref, 1 - core)):
+        for at, size, ahead, skip in ((0, 128, 0, 0), (128, 128, 3, 0), (256, 128, 1, 0), (384, 64, 2, 0), (448, 64, 2, 64)):
+            to = tile * 512 + lax.rem(x + ahead, 4) * 128 + skip
+            panel[pl.ds(pl.multiple_of(to, 64), size), :] = ref[at : at + size, :]
+
+    spread_rows(pivots_ref, g_high, g_low)
+    take_high, take_low = split(take_ref[...])
+    for n in range(4):
+        at = slice(256 * n, 256 * n + 256)
+        u_ref[:, at] = dot3(take_high, take_low, g_high[:, at], g_low[:, at])
+    for n in range(4):
+        at = slice(256 * n, 256 * n + 256)
+        part_high[:, at], part_low[:, at] = split(u_ref[:, at])
+
+    inv_high, inv_low = split(inv_ref[...])
+    keep_high, keep_low = split(keep_ref[...])
+
+    @pl.loop(0, 4)
+    def _(b):
+        at = pl.ds(pl.multiple_of(b * 256, 256), 256)
+        high, low = split(panel[at, :])
+        high, low = split(dot3(high, low, inv_high, inv_low))
+        l_high[at, :], l_low[at, :] = high, low
+        lw_high[at, :], lw_low[at, :] = split(dot3(high, low, keep_high, keep_low))
+
+    copy.wait()
+
+    @pl.loop(0, 4)
+    def _(b):
+        at = pl.ds(pl.multiple_of(b * 256, 256), 256)
+        high, low = l_high[at, :], l_low[at, :]
+        for n in range(4):
+            cols = slice(256 * n, 256 * n + 256)
+            product = dot3(high, low, part_high[:, cols], part_low[:, cols])
+            for part in range(2):
+                to = pl.ds(pl.multiple_of(b * 2048, 2048) + 2 * n + part, 256, stride=8)
+                m_ref[to, :] = m_ref[to, :] - product[:, 128 * part : 128 * part + 128]
+
+    @pl.when(rows_ref[2] == 0)
+    def _():
+        for l in range(4):
+            cols = slice(128 * l, 128 * l + 128)
+            m_ref[pl.ds(2 * l, 1024, stride=8), :] = l_high[:, cols].astype(jnp.float32) + l_low[:, cols].astype(jnp.float32)
+
+    @pl.when(rows_ref[1] == 0)
+    def _():
+        for sub in range(8):
+            m_ref[pl.ds(sub, 512, stride=8), :] = u_ref[:, 128 * sub : 128 * sub + 128]
+        lw_high[:512, :], lw_low[:512, :] = -keep_high, -keep_low
+
+
+def early(rows, half, other, inv_upper, pivots, take, keep, x):
+    part = jax.ShapeDtypeStruct((1024, 512), jnp.bfloat16)
+    upper = jax.ShapeDtypeStruct((512, 1024), jnp.bfloat16)
+    half_scratch = pltpu.VMEM((1024, 512), jnp.bfloat16)
+    return pl.pallas_call(
+        early_kernel,
+        out_shape=[jax.ShapeDtypeStruct((8192, 128), jnp.float32), part, part, upper, upper],
+        in_specs=whole(pltpu.SMEM, 1) + whole(pltpu.VMEM, 6) + whole(pl.ANY, 1),
+        out_specs=whole(pltpu.VMEM, 5),
+        scratch_shapes=[
+            pltpu.VMEM((1024, 512), jnp.float32),
+            half_scratch,
+            half_scratch,
+            pltpu.VMEM((16 * CAP, 1024), jnp.bfloat16),
+            pltpu.VMEM((16 * CAP, 1024), jnp.bfloat16),
+            pltpu.VMEM((512, 1024), jnp.float32),
+            pltpu.SemaphoreType.DMA(()),
+        ],
+        compiler_params=pltpu.CompilerParams(vmem_limit_bytes=VMEM),
+        cost_estimate=pl.CostEstimate(flops=9 * 10**9, bytes_accessed=24 * MIB, transcendentals=0),
+        name="early",
+    )(rows, half, other, inv_upper, pivots, take, keep, x)
+
+
+def patch_kernel(rows_ref, sent_ref, inv_ref, keep_ref, part_high, part_low, out_ref, lw_high, lw_low):
+    high, low = split(dot3(*split(sent_ref[...]), *split(inv_ref[...])))
+    lw_high[...], lw_low[...] = split(dot3(high, low, *split(keep_ref[...])))
+    product = dot3(high, low, part_high[...], part_low[...])
+    for sub in range(8):
+        out_ref[pl.ds(sub, CAP, stride=8), :] = -product[:, 128 * sub : 128 * sub + 128]
+
+    @pl.when(rows_ref[2] == 0)
+    def _():
+        lower = high.astype(jnp.float32) + low.astype(jnp.float32)
+        for l in range(4):
+            out_ref[pl.ds(2 * l, CAP, stride=8), :] = lower[:, 128 * l : 128 * l + 128]
+
+
+def patch(rows, sent, inv_upper, keep, part_high, part_low):
+    lw = jax.ShapeDtypeStruct((CAP, 512), jnp.bfloat16)
+    return pl.pallas_call(
+        patch_kernel,
+        out_shape=[jax.ShapeDtypeStruct((CAP * 8, 128), jnp.float32), lw, lw],
+        in_specs=whole(pltpu.SMEM, 1) + whole(pltpu.VMEM, 5),
+        out_specs=whole(pltpu.VMEM, 3),
+        compiler_params=pltpu.CompilerParams(vmem_limit_bytes=VMEM),
+        cost_estimate=pl.CostEstimate(flops=10**9, bytes_accessed=4 * MIB, transcendentals=0),
+        name="patch",
+    )(rows, sent, inv_upper, keep, part_high, part_low)
+
+
+def late_kernel(
+    rows_ref, m_ref, lw_high, lw_low, new_ref, new_high, new_low, x_all, top_all, out_ref, top, g_high, g_low, new, load
+):
+    block = pl.program_id(0)
+    parity = lax.rem(lax.broadcasted_iota(jnp.int32, (8, 128), 0), 2)
+
+    @pl.when(block == 0)
+    def _():
+        copies = [pltpu.make_async_copy(ref.at[pl.ds(0, 4096)], top, load) for ref in (x_all, top_all)]
+        for owned, copy in zip((rows_ref[1] == 0, rows_ref[1] != 0), copies):
+            pl.when(owned)(copy.start)
+        for owned, copy in zip((rows_ref[1] == 0, rows_ref[1] != 0), copies):
+            pl.when(owned)(copy.wait)
+        spread_rows(top, g_high, g_low)
+        product = dot3(new_high[...], new_low[...], g_high[...], g_low[...])
+        for sub in range(8):
+            new[pl.ds(sub, CAP, stride=8), :] = product[:, 128 * sub : 128 * sub + 128]
+
+    high, low = lw_high[...], lw_low[...]
+    solved = (rows_ref[2] == 0) & ((rows_ref[1] != 0) | (block >= 2))
+    for n in range(4):
+        cols = slice(256 * n, 256 * n + 256)
+        product = dot3(high, low, g_high[:, cols], g_low[:, cols])
+        for part in range(2):
+            at = pl.ds(2 * n + part, 256, stride=8)
+            value = product[:, 128 * part : 128 * part + 128]
+            if part == 0:
+                value = jnp.where(solved, 0.0, value)
+            out_ref[at, :] = m_ref[at, :] - value
+
+    @pl.loop(0, rows_ref[0])
+    def _(k):
+        row = rows_ref[8 + k] - block * 256
+
+        @pl.when((row >= 0) & (row < 256))
+        def _():
+            at = pl.ds(pl.multiple_of(k * 8, 8), 8)
+            change = top[pl.ds(pl.multiple_of(rows_ref[8 + CAP + k] * 8, 8), 8), :] - new[at, :]
+            change = jnp.where((parity == 1) | (rows_ref[2] != 0), change, 0.0)
+            out_ref[pl.ds(pl.multiple_of(row * 8, 8), 8), :] = new_ref[at, :] + change
+
+
+def late(rows, m, lw_high, lw_low, new, new_high, new_low, x, top):
+    block = lambda *shape: pl.BlockSpec(shape, lambda i, *_: (i, 0))
+    return pl.pallas_call(
+        late_kernel,
+        out_shape=jax.ShapeDtypeStruct((8192, 128), jnp.float32),
+        grid_spec=pltpu.PrefetchScalarGridSpec(
+            num_scalar_prefetch=1,
+            grid=(4,),
+            in_specs=[block(2048, 128), block(256, 512), block(256, 512)]
+            + whole(pltpu.VMEM, 3)
+            + whole(pl.ANY, 2),
+            out_specs=block(2048, 128),
+            scratch_shapes=[pltpu.VMEM((4096, 128), jnp.float32)]
+            + [pltpu.VMEM((512, 1024), jnp.bfloat16)] * 2
+            + [pltpu.VMEM((CAP * 8, 128), jnp.float32), pltpu.SemaphoreType.DMA(())],
+        ),
+        compiler_params=pltpu.CompilerParams(vmem_limit_bytes=VMEM),
+        cost_estimate=pl.CostEstimate(flops=3 * 2 * 1024 * 512 * 1024, bytes_accessed=12 * MIB, transcendentals=0),
+        name="late",
+    )(rows, m, lw_high, lw_low, new, new_high, new_low, x, top)
+
+
+def x_shift(value, by):
+    return lax.ppermute(value, "col", [(i, i // 8 * 8 + (i // 2 + by) % 4 * 2 + i % 2) for i in range(16)])
+
+
+def swap(value, axis):
+    return lax.ppermute(value, axis, [(i, i ^ 1) for i in range(16)])
+
+
+def gather_layers(piece):
+    groups = [[2 * i + j for i in range(LAYERS)] for j in range(2)]
+    return lax.all_gather(piece, "row", axis_index_groups=groups, axis=0, tiled=True)
+
+
+def across(value, col):
+    value = jnp.where(col == 0, value, 0.0)
+    value = value + lax.ppermute(value, "col", [(0, 1)])
+    got = [lax.ppermute(value, "col", [(0, 2 * to), (1, 2 * to + 1)]) for to in (1, 3, 2)]
+    value = value + got[0] + got[1] + got[2]
+    return value + lax.ppermute(value, "col", [(i, i + 8) for i in range(8)])
+
+
+def scatter_panel(first, second, col, before, between):
+    core, x = col % 2, col // 2 % 4
+    half = jnp.where(core == 0, first, lax.ppermute(second, "col", [(0, 1)])) + 0.0 * before[0, 0]
+    mine = jnp.where(x == 0, half[:128], 0.0 * between[0, 0])
+    got = [
+        lax.ppermute(half[128 * to : 128 * to + 128], "col", [(0, 2 * to), (1, 2 * to + 1)])
+        for to in (1, 3, 2)
+    ]
+    return jnp.where(col < 8, mine + got[0] + got[1] + got[2], 0.0)
+
+
+def gather_panel(mine):
+    mine = mine + lax.ppermute(mine, "col", [(i, i + 8) for i in range(8)])
+    up, down = x_shift(mine, 1), x_shift(mine, -1)
+    last = [x_shift(up[:64], 1), x_shift(down[64:], -1)]
+    return jnp.concatenate([mine, up, down] + last), last[0][0, 0] + last[1][0, 0]
+
+
+def few_pivots(matrix, pivot_rows, inv_lower, inv_upper, owner, rank):
+    best = lax.Precision.HIGHEST
+    row, col = lax.axis_index("row"), lax.axis_index("col")
+    z, y = row // 2, row % 2
+    x2 = as_rows(matrix).reshape(8192, 128)
+
+    index = jnp.arange(TILE, dtype=jnp.int32)
+    slots = jnp.arange(CAP, dtype=jnp.int32)
+    here = pivot_rows // TILE // 16 * TILE + pivot_rows % TILE
+    mine = (owner[:, None] == row) & (rank[:, None] == slots[None, :])
+    at_rows = jnp.sum(jnp.where(mine, here[:, None], 0), axis=0)
+    from_top = jnp.sum(jnp.where(mine, index[:, None], 0), axis=0)
+    count = jnp.minimum(jnp.sum((owner == row).astype(jnp.int32)), CAP)
+    head = jnp.stack([count, row, col] + [jnp.int32(0)] * 5).astype(jnp.int32)
+    rows = jnp.concatenate([head, at_rows, from_top])
+    key = jnp.where(owner < 0, -1, owner * CAP + jnp.minimum(rank, CAP - 1))[None]
+    first, second, picked, *packed = prepare(rows, key, x2)
+
+    paired = swap(picked, "row")
+    paired = jnp.concatenate([jnp.where(y == 0, picked, paired), jnp.where(y == 0, paired, picked)])
+    pivots = gather_layers(paired)
+
+    handed = [lax.ppermute(value, "row", [(0, 1)]) for value in packed[LAYERS:]]
+    odd = {}
+    for group, value in zip((FAR, NEAR), handed):
+        odd.update({k: value[320 * at : 320 * at + 320] for at, k in enumerate(group)})
+
+    half, token = gather_panel(scatter_panel(first, second, col, *handed))
+    other_half = swap(half, "col")
+
+    pieces = [jnp.where(row == 0, packed[k], odd[k]) for k in range(LAYERS)]
+    piece = jnp.where(z == 0, pieces[0], 0.0 * token)
+    for to in FAR + NEAR[:-1]:
+        piece = piece + lax.ppermute(pieces[to], "row", [(0, 2 * to), (1, 2 * to + 1)])
+    other = swap(piece[:256], "row")
+    tops = gather_layers(
+        jnp.concatenate([jnp.where(y == 0, piece[:256], other), jnp.where(y == 0, other, piece[:256])])
+    )
+
+    extra = piece.reshape(40, 4, 2, 128)
+    sent = jnp.concatenate([extra[:, :, 0], extra[32:, :, 1]]).reshape(CAP, TILE)
+    sent = across(sent, col)
+
+    take = (key[0][:, None] == jnp.arange(16 * CAP, dtype=jnp.int32)[None, :]) & (rank < CAP)[:, None]
+    taken = jnp.dot(inv_lower, take.astype(jnp.float32), precision=best, preferred_element_type=jnp.float32)
+    kept = jnp.where((owner < 0)[None, :], inv_lower, 0.0)
+    m, lw_high, lw_low, part_high, part_low = early(rows, half, other_half, inv_upper, pivots, taken, kept, x2)
+    new, new_high, new_low = patch(rows, sent, inv_upper, kept, part_high, part_low)
+    out = late(rows, m, lw_high, lw_low, new, new_high, new_low, x2, tops)
+    return as_matrix(out.reshape(1024, 8, 128))
+
+
+def local(matrix, pivot_rows, inv_lower, inv_upper):
+    moved = pivot_rows >= TILE
+    owner = jnp.where(moved, pivot_rows // TILE % 16, -1)
+    index = jnp.arange(TILE, dtype=jnp.int32)
+    before = (owner[:, None] == owner[None, :]) & (index[None, :] < index[:, None])
+    rank = jnp.sum(before.astype(jnp.int32), axis=1)
+    crowded = jnp.max(jnp.where(moved, rank, 0)) >= CAP
+    out = few_pivots(matrix, pivot_rows, inv_lower, inv_upper, owner, rank)
+
+    def body(state):
+        return jnp.bool_(False), any_pivots(matrix, pivot_rows, inv_lower, inv_upper)
+
+    return lax.while_loop(lambda state: state[0], body, (crowded, out))[1]
+
+
 def solution(mesh):
     return jax.shard_map(
         local,

time: 421 us -> 164 us (0.39); the launches traced: 415 us -> 163 us
  waiting for transfers between devices: 339 us -> 57.6 us
  Pallas kernels: 0 us -> 41.8 us
  starting transfers between devices: 0.22 us -> 24.9 us
  local copies, waits for them, and re-layouts: 27.9 us -> 6.82 us
  matrix products: 19.6 us -> 2.82 us
  between operations: 13.5 us -> 17.9 us
    psum x2 -> x0, waiting for transfers between devices: 339 us -> none  [spread(): return lax.psum(block, axis)]
    ppermute x0 -> x26, waiting for transfers between devices: none -> 57.6 us  [the longest x7 21.5 us: few_pivots(): lax.ppermute(pieces[to], 'row', [(0, 2 * to), (1, 2 * to + 1)])]
    pallas_call x0 -> x4, Pallas kernels: none -> 41.8 us  [the longest x1 19.1 us: early(): pl.pallas_call(early_kernel, out_shape=[jax.ShapeDtypeStruct((8192, 128),...]
    ppermute x0 -> x26, starting transfers between devices: none -> 24.8 us  [the longest x4 7.63 us: x_shift(): lax.ppermute(value, 'col', [(i, i // 8 * 8 + (i // 2 + by) % 4 * 2 + i %...]
    dot_general x3 -> x1, matrix products: 19.6 us -> 2.82 us  [few_pivots(): jnp.dot(inv_lower, take.astype(jnp.float32), precision=best, preferred_el...]
    gather x2 -> x0, local copies, waits for them, and re-layouts: 13 us -> none  [the longest x1 7.95 us: local(): swapped = jnp.where(has_source[:, None], former_top[source], matrix_here)]
    reshape x1 -> x0, local copies, waits for them, and re-layouts: 6.57 us -> none  [local(): return result.reshape(tiles_down, tile_width, tiles_across, tile_width)]
    unnamed x12 -> x31, local copies, waits for them, and re-layouts: 8.36 us -> 2.18 us
  transfers between devices with their start and end apart: 2 -> 28, of which waited for: 2 -> 7; matrix products, arithmetic and copies ran while one was open for 2% -> 9% of each run, Pallas kernels for 0% -> 14%
where the time goes in v1:
time: 164 us; the launch traced here: 163 us
  waiting for transfers between devices  57.6 us (35%)
  Pallas kernels  41.8 us (25%)
  starting transfers between devices  24.9 us (15%)
  between operations  17.9 us (11%)
  other arithmetic  11.1 us (7%)
  local copies, waits for them, and re-layouts  6.82 us (4%)
  matrix products  2.82 us (2%)
    ppermute x7, waiting for transfers between devices, few_pivots(): lax.ppermute(pieces[to], 'row', [(0, 2 * to), (1, 2 * to + 1)])  21.5 us
    pallas_call x1, Pallas kernels, early(): pl.pallas_call(early_kernel, out_shape=[jax.ShapeDtypeStruct((8192, 128),...  19.1 us
    pallas_call x1, Pallas kernels, late(): pl.pallas_call(late_kernel, out_shape=jax.ShapeDtypeStruct((8192, 128), j...  13.2 us
    ppermute x1, waiting for transfers between devices, gather_panel(): mine = mine + lax.ppermute(mine, 'col', [(i, i + 8) for i in range(8)])  12.7 us
    ppermute x3, waiting for transfers between devices, swap(): return lax.ppermute(value, axis, [(i, i ^ 1) for i in range(16)])  11.1 us
    ppermute x1, waiting for transfers between devices, across(): return value + lax.ppermute(value, 'col', [(i, i + 8) for i in range(8)])  9.45 us
    ppermute x4, starting transfers between devices, x_shift(): lax.ppermute(value, 'col', [(i, i // 8 * 8 + (i // 2 + by) % 4 * 2 + i %...  7.63 us
    pallas_call x1, Pallas kernels, prepare(): pl.pallas_call(prepare_kernel, out_shape=[half, half, picked] + [piece] *...  5.56 us
  transfers between devices with their start and end apart: 28, of which 7 were waited for; matrix products, arithmetic and copies ran while one was open for 9% of the time, Pallas kernels for 14%

profile of v1, /device:TPU:58, one launch (start us, length us, event | category | flops | bytes accessed | tf_op | source)
XLA Modules:
  0.0 163.1 jit_solution(9260551041005274977)
XLA Ops:
  7.5 1.9 %convert_reduce_fusion.1 = (s32[]{:T(128)}, pred[512]{0:T(512)(128)(4,1)S(1)}, s32[512]{0:T(512)}, s32[512]{0:T(512)S(1)}) fusion(s32[512]{0:T(512)S(1)} %get-tuple-element.95, s32[]{:T(128)} %axis_index.51, s32[512]{0:T(512)S(1)} %convert_reduce_fusion, s32[512]{0:T(512)} %param.7), kind=kLoop, calls=%fused_computation.134 | loop fusion | flops 22527 | bytes 10760 | tf_op jit(solution)/shard_map/reduce_sum | solution.py:387
  10.9 5.6 %prepare.1 = (f32[512,512]{1,0:T(8,128)}, f32[512,512]{1,0:T(8,128)}, f32[384,128]{1,0:T(8,128)}, f32[320,128]{1,0:T(8,128)}, f32[320,128]{1,0:T(8,128)}, /*inde...) custom-call(s32[104]{0:T(128)} %concatenate.26.rows_ref, ...), custom_call_target="tpu_custom_call" | custom-call | flops 2000000000 | bytes 10485760 | tf_op jit(solution)/shard_map/prepare/pallas_call | solution.py:143
  17.3 6.1 %collective-permute-done.12 = f32[384,128]{1,0:T(8,128)S(1)} collective-permute-done((f32[384,128]{1,0:T(8,128)}, f32[384,128]{1,0:T(8,128)S(1)}, u32[]{:S(2)}, u32[]{:S(2)}) %collective-permute-start.12) | collective-permute-done | bytes 196640 | tf_op jit(solution)/shard_map/ppermute | solution.py:341
  23.4 1.0 broadcast_select_fusion.4
  26.6 1.6 collective-permute-start.2
  32.1 1.2 slice.116
  34.1 1.4 collective-permute-start.6
  35.6 12.7 %collective-permute-done.6 = f32[128,512]{1,0:T(8,128)S(1)} collective-permute-done((f32[128,512]{1,0:T(8,128)S(1)}, f32[128,512]{1,0:T(8,128)S(1)}, u32[]{:S(2)}, u32[]{:S(2)}) %collective-permute-start.6) | collective-permute-done | bytes 262176 | tf_op jit(solution)/shard_map/ppermute | solution.py:369
  49.0 3.2 %collective-permute-start.8 = (f32[128,512]{1,0:T(8,128)S(1)}, f32[128,512]{1,0:T(8,128)S(1)}, u32[]{:S(2)}, u32[]{:S(2)}) collective-permute-start(f32[128,512]{1,0:T(8,128)S(1)} %get-tuple-element.98), channel_id=1, source_target_pairs={{0,6},{1,7},{2,0},{3,1},{4,2},{5,3},{6,4},{7,5},{8,14},{9,15},{10,... | collective-permute-start | bytes 786440 | tf_op jit(solution)/shard_map/ppermute | solution.py:337
  52.3 1.9 %collective-permute-start.7 = (f32[128,512]{1,0:T(8,128)S(1)}, f32[128,512]{1,0:T(8,128)S(1)}, u32[]{:S(2)}, u32[]{:S(2)}) collective-permute-start(f32[128,512]{1,0:T(8,128)S(1)} %get-tuple-element.98), channel_id=1, source_target_pairs={{0,2},{1,3},{2,4},{3,5},{4,6},{5,7},{6,0},{7,1},{8,10},{9,11},{10,... | collective-permute-start | bytes 786440 | tf_op jit(solution)/shard_map/ppermute | solution.py:337
  56.3 2.5 %collective-permute-done.8 = f32[128,512]{1,0:T(8,128)S(1)} collective-permute-done((f32[128,512]{1,0:T(8,128)S(1)}, f32[128,512]{1,0:T(8,128)S(1)}, u32[]{:S(2)}, u32[]{:S(2)}) %collective-permute-start.8) | collective-permute-done | bytes 262176 | tf_op jit(solution)/shard_map/ppermute | solution.py:337
  59.0 2.4 %collective-permute-start.9 = (f32[64,512]{1,0:T(8,128)S(1)}, f32[64,512]{1,0:T(8,128)S(1)}, u32[]{:S(2)}, u32[]{:S(2)}) collective-permute-start(f32[64,512]{1,0:T(8,128)S(1)} %slice.120), channel_id=1, source_target_pairs={{0,2},{1,3},{2,4},{3,5},{4,6},{5,7},{6,0},{7,1},{8,10},{9,11},{10,... | collective-permute-start | bytes 393224 | tf_op jit(solution)/shard_map/ppermute | solution.py:337
  61.4 1.1 slice_select_fusion.5
  64.9 1.3 collective-permute-start.18
  68.6 21.5 %collective-permute-done.18 = f32[320,128]{1,0:T(8,128)S(1)} collective-permute-done((f32[320,128]{1,0:T(8,128)S(1)}, f32[320,128]{1,0:T(8,128)S(1)}, u32[]{:S(2)}, u32[]{:S(2)}) %collective-permute-start.18) | collective-permute-done | bytes 163872 | tf_op jit(solution)/shard_map/ppermute | solution.py:408
  90.1 1.0 fusion.46
  91.2 5.0 %collective-permute-done.25 = f32[256,128]{1,0:T(8,128)S(1)} collective-permute-done((f32[256,128]{1,0:T(8,128)S(1)}, f32[256,128]{1,0:T(8,128)S(1)}, u32[]{:S(2)}, u32[]{:S(2)}) %collective-permute-start.25) | collective-permute-done | bytes 131104 | tf_op jit(solution)/shard_map/ppermute | solution.py:341
  100.8 2.8 %fusion.29.take_ref = f32[512,768]{1,0:T(8,128)} fusion(f32[512,512]{1,0:T(8,128)S(1)} %copy-done.3, s32[512]{0:T(512)S(1)} %copy-done.16, pred[512]{0:T(512)(128)(4,1)S(1)} %broadcast_compare_fusion.1), kind=kOutput, calls=%fused_computation.69 | convolution fusion | flops 2416705536 | bytes 2624000 | tf_op jit(solution)/shard_map/dot_general | solution.py:419
  106.1 1.1 broadcast_select_fusion.2.keep_ref
  107.2 1.3 collective-permute-start.24
  109.7 9.5 %collective-permute-done.24 = f32[48,512]{1,0:T(8,128)S(1)} collective-permute-done((f32[48,512]{1,0:T(8,128)S(1)}, f32[48,512]{1,0:T(8,128)S(1)}, u32[]{:S(2)}, u32[]{:S(2)}) %collective-permute-start.24) | collective-permute-done | bytes 98336 | tf_op jit(solution)/shard_map/ppermute | solution.py:354
  119.8 19.1 %early.1 = (f32[8192,128]{1,0:T(8,128)}, bf16[1024,512]{1,0:T(8,128)(2,1)}, bf16[1024,512]{1,0:T(8,128)(2,1)}, bf16[512,1024]{1,0:T(8,128)(2,1)}, bf16[512,1024]{1,0:T(8,128)(2,1)}) custom-call(s32[104]{0:T(128)} %concatenate.26.rows_ref, f32[512,512]{1,0:T(8,128)} %constant_dynamic-update-slice_fusion.half_ref, ...), custom_call_target="tpu_custom_call" | custom-call | flops 8999999488 | bytes 25165824 | tf_op jit(solution)/shard_map/early/pallas_call | solution.py:225
  138.9 3.9 %patch.1 = (f32[384,128]{1,0:T(8,128)}, bf16[48,512]{1,0:T(8,128)(2,1)}, bf16[48,512]{1,0:T(8,128)(2,1)}) custom-call(s32[104]{0:T(128)} %concatenate.26.rows_ref, f32[48,512]{1,0:T(8,128)} %add.241.sent_ref, f32[512,512]{1,0:T(8,128)S(1)} %copy-done.5, f32[512,512]{1,0:T(8,128)} %broadcast_select_fusion.2.keep_ref, ...), custom_call_target="tpu_custom_call" | custom-call | flops 1000000000 | bytes 4194304 | tf_op jit(solution)/shard_map/patch/pallas_call | solution.py:261
  142.8 13.2 %late.1 = f32[8192,128]{1,0:T(8,128)} custom-call(s32[104]{0:T(128)} %concatenate.26.rows_ref, f32[8192,128]{1,0:T(8,128)} %get-tuple-element.61.m_ref, bf16[1024,512]{1,0:T(8,128)(2,1)} %get-tuple-element.62.lw_high, bf16[1024,512]{1,0:T(8,128)(2,1)} %get-tuple-element.63.lw_low, f32[384,128]{1,0:T(8,128)} %get-tuple-element.74.new_ref, ...), custom_call_target="tpu_custom_call" | custom-call | flops 3221225472 | bytes 12582912 | tf_op jit(solution)/shard_map/late/pallas_call | solution.py:316
  (105 shorter events, 23.1 us)
Async XLA Ops:
  6.5 113.2 %all-gather.3.cloned.1.call-start = ((), (), s32[]{:S(2)}) async-start(), calls=%async_computation.2 | async-start | bytes 3538944 | tf_op jit(solution)/shard_map/all_gather | solution.py:346
  16.4 6.9 %collective-permute-start.12 = (f32[384,128]{1,0:T(8,128)}, f32[384,128]{1,0:T(8,128)S(1)}, u32[]{:S(2)}, u32[]{:S(2)}) collective-permute-start(f32[384,128]{1,0:T(8,128)} %get-tuple-element.60), channel_id=1, source_target_pairs={{0,16},{16,0},{32,48},{48,32},{64,80},{80,64},{96,112},{112,96},{1... | collective-permute-start | bytes 589832 | tf_op jit(solution)/shard_map/ppermute | solution.py:341
  25.1 117.7 %all-gather.5.cloned.1.call-start = ((), (), s32[]{:S(2)}) async-start(), calls=%async_computation.3 | async-start | bytes 2359296 | tf_op jit(solution)/shard_map/all_gather | solution.py:346
  25.2 4.3 %collective-permute-start = (f32[512,512]{1,0:T(8,128)}, f32[512,512]{1,0:T(8,128)S(1)}, u32[]{:S(2)}, u32[]{:S(2)}) collective-permute-start(f32[512,512]{1,0:T(8,128)} %get-tuple-element.57), channel_id=1, source_target_pairs={{0,1},{16,17},{32,33},{48,49},{64,65},{80,81},{96,97},{112,113},{1... | collective-permute-start | bytes 3145736 | tf_op jit(solution)/shard_map/ppermute | solution.py:359
  26.6 5.5 %collective-permute-start.2 = (f32[1280,128]{1,0:T(8,128)}, f32[1280,128]{1,0:T(8,128)}, u32[]{:S(2)}, u32[]{:S(2)}) collective-permute-start(f32[1280,128]{1,0:T(8,128)} %get-tuple-element.59), channel_id=1, source_target_pairs={{0,16},{1,17},{2,18},{3,19},{4,20},{5,21},{6,22},{7,23},{8,24},{9,... | collective-permute-start | bytes 1966088 | tf_op jit(solution)/shard_map/ppermute | solution.py:397
  29.9 4.1 %collective-permute-start.3 = (f32[128,512]{1,0:T(8,128)S(1)}, f32[128,512]{1,0:T(8,128)S(1)}, u32[]{:S(2)}, u32[]{:S(2)}) collective-permute-start(f32[128,512]{1,0:T(8,128)S(1)} %get-tuple-element.103), channel_id=1, source_target_pairs={{0,2},{1,3},{16,18},{17,19},{32,34},{33,35},{48,50},{49,51},{64,66... | collective-permute-start | bytes 786440 | tf_op jit(solution)/shard_map/ppermute | solution.py:362
  30.7 3.3 %collective-permute-start.5 = (f32[128,512]{1,0:T(8,128)S(1)}, f32[128,512]{1,0:T(8,128)S(1)}, u32[]{:S(2)}, u32[]{:S(2)}) collective-permute-start(f32[128,512]{1,0:T(8,128)S(1)} %get-tuple-element.104), channel_id=1, source_target_pairs={{0,4},{1,5},{16,20},{17,21},{32,36},{33,37},{48,52},{49,53},{64,68... | collective-permute-start | bytes 786440 | tf_op jit(solution)/shard_map/ppermute | solution.py:362
  34.1 14.1 %collective-permute-start.6 = (f32[128,512]{1,0:T(8,128)S(1)}, f32[128,512]{1,0:T(8,128)S(1)}, u32[]{:S(2)}, u32[]{:S(2)}) collective-permute-start(f32[128,512]{1,0:T(8,128)S(1)} %fusion.38), channel_id=1, source_target_pairs={{0,8},{1,9},{2,10},{3,11},{4,12},{5,13},{6,14},{7,15},{16,24},{17,... | collective-permute-start | bytes 786440 | tf_op jit(solution)/shard_map/ppermute | solution.py:369
  49.0 9.8 %collective-permute-start.8 = (f32[128,512]{1,0:T(8,128)S(1)}, f32[128,512]{1,0:T(8,128)S(1)}, u32[]{:S(2)}, u32[]{:S(2)}) collective-permute-start(f32[128,512]{1,0:T(8,128)S(1)} %get-tuple-element.98), channel_id=1, source_target_pairs={{0,6},{1,7},{2,0},{3,1},{4,2},{5,3},{6,4},{7,5},{8,14},{9,15},{10,... | collective-permute-start | bytes 786440 | tf_op jit(solution)/shard_map/ppermute | solution.py:337
  52.3 6.7 %collective-permute-start.7 = (f32[128,512]{1,0:T(8,128)S(1)}, f32[128,512]{1,0:T(8,128)S(1)}, u32[]{:S(2)}, u32[]{:S(2)}) collective-permute-start(f32[128,512]{1,0:T(8,128)S(1)} %get-tuple-element.98), channel_id=1, source_target_pairs={{0,2},{1,3},{2,4},{3,5},{4,6},{5,7},{6,0},{7,1},{8,10},{9,11},{10,... | collective-permute-start | bytes 786440 | tf_op jit(solution)/shard_map/ppermute | solution.py:337
  54.3 8.2 %collective-permute-start.13 = (f32[320,128]{1,0:T(8,128)S(1)}, f32[320,128]{1,0:T(8,128)S(1)}, u32[]{:S(2)}, u32[]{:S(2)}) collective-permute-start(f32[320,128]{1,0:T(8,128)S(1)} %get-tuple-element.106), channel_id=1, source_target_pairs={{0,128},{16,144},{1,129},{17,145},{2,130},{18,146},{3,131},{19,147... | collective-permute-start | bytes 491528 | tf_op jit(solution)/shard_map/ppermute | solution.py:408
  55.0 8.2 %collective-permute-start.16 = (f32[320,128]{1,0:T(8,128)S(1)}, f32[320,128]{1,0:T(8,128)S(1)}, u32[]{:S(2)}, u32[]{:S(2)}) collective-permute-start(f32[320,128]{1,0:T(8,128)S(1)} %get-tuple-element.107), channel_id=1, source_target_pairs={{0,64},{16,80},{1,65},{17,81},{2,66},{18,82},{3,67},{19,83},{4,68}... | collective-permute-start | bytes 491528 | tf_op jit(solution)/shard_map/ppermute | solution.py:408
  55.6 13.0 %collective-permute-start.15 = (f32[320,128]{1,0:T(8,128)S(1)}, f32[320,128]{1,0:T(8,128)S(1)}, u32[]{:S(2)}, u32[]{:S(2)}) collective-permute-start(f32[320,128]{1,0:T(8,128)S(1)} %get-tuple-element.108), channel_id=1, source_target_pairs={{0,160},{16,176},{1,161},{17,177},{2,162},{18,178},{3,163},{19,179... | collective-permute-start | bytes 491528 | tf_op jit(solution)/shard_map/ppermute | solution.py:408
  58.8 5.3 %collective-permute-start.10 = (f32[64,512]{1,0:T(8,128)S(1)}, f32[64,512]{1,0:T(8,128)S(1)}, u32[]{:S(2)}, u32[]{:S(2)}) collective-permute-start(f32[64,512]{1,0:T(8,128)S(1)} %slice.121), channel_id=1, source_target_pairs={{0,6},{1,7},{2,0},{3,1},{4,2},{5,3},{6,4},{7,5},{8,14},{9,15},{10,... | collective-permute-start | bytes 393224 | tf_op jit(solution)/shard_map/ppermute | solution.py:337
  59.0 5.9 %collective-permute-start.9 = (f32[64,512]{1,0:T(8,128)S(1)}, f32[64,512]{1,0:T(8,128)S(1)}, u32[]{:S(2)}, u32[]{:S(2)}) collective-permute-start(f32[64,512]{1,0:T(8,128)S(1)} %slice.120), channel_id=1, source_target_pairs={{0,2},{1,3},{2,4},{3,5},{4,6},{5,7},{6,0},{7,1},{8,10},{9,11},{10,... | collective-permute-start | bytes 393224 | tf_op jit(solution)/shard_map/ppermute | solution.py:337
  62.5 6.1 %collective-permute-start.14 = (f32[320,128]{1,0:T(8,128)S(1)}, f32[320,128]{1,0:T(8,128)S(1)}, u32[]{:S(2)}, u32[]{:S(2)}) collective-permute-start(f32[320,128]{1,0:T(8,128)S(1)} %get-tuple-element.109), channel_id=1, source_target_pairs={{0,96},{16,112},{1,97},{17,113},{2,98},{18,114},{3,99},{19,115},{4... | collective-permute-start | bytes 491528 | tf_op jit(solution)/shard_map/ppermute | solution.py:408
  63.2 5.4 %collective-permute-start.17 = (f32[320,128]{1,0:T(8,128)S(1)}, f32[320,128]{1,0:T(8,128)S(1)}, u32[]{:S(2)}, u32[]{:S(2)}) collective-permute-start(f32[320,128]{1,0:T(8,128)S(1)} %get-tuple-element.110), channel_id=1, source_target_pairs={{0,192},{16,208},{1,193},{17,209},{2,194},{18,210},{3,195},{19,211... | collective-permute-start | bytes 491528 | tf_op jit(solution)/shard_map/ppermute | solution.py:408
  64.2 4.4 %collective-permute-start.19 = (f32[320,128]{1,0:T(8,128)S(1)}, f32[320,128]{1,0:T(8,128)S(1)}, u32[]{:S(2)}, u32[]{:S(2)}) collective-permute-start(f32[320,128]{1,0:T(8,128)S(1)} %get-tuple-element.111), channel_id=1, source_target_pairs={{0,224},{16,240},{1,225},{17,241},{2,226},{18,242},{3,227},{19,243... | collective-permute-start | bytes 491528 | tf_op jit(solution)/shard_map/ppermute | solution.py:408
  64.9 25.2 %collective-permute-start.18 = (f32[320,128]{1,0:T(8,128)S(1)}, f32[320,128]{1,0:T(8,128)S(1)}, u32[]{:S(2)}, u32[]{:S(2)}) collective-permute-start(f32[320,128]{1,0:T(8,128)S(1)} %get-tuple-element.112), channel_id=1, source_target_pairs={{0,32},{16,48},{1,33},{17,49},{2,34},{18,50},{3,35},{19,51},{4,36}... | collective-permute-start | bytes 491528 | tf_op jit(solution)/shard_map/ppermute | solution.py:408
  91.1 5.1 %collective-permute-start.25 = (f32[256,128]{1,0:T(8,128)S(1)}, f32[256,128]{1,0:T(8,128)S(1)}, u32[]{:S(2)}, u32[]{:S(2)}) collective-permute-start(f32[256,128]{1,0:T(8,128)S(1)} %slice.134), channel_id=1, source_target_pairs={{0,16},{16,0},{32,48},{48,32},{64,80},{80,64},{96,112},{112,96},{1... | collective-permute-start | bytes 393224 | tf_op jit(solution)/shard_map/ppermute | solution.py:341
  99.7 20.0 %collective-permute-start.11 = (f32[512,512]{1,0:T(8,128)}, f32[512,512]{1,0:T(8,128)}, u32[]{:S(2)}, u32[]{:S(2)}) collective-permute-start(f32[512,512]{1,0:T(8,128)} %constant_dynamic-update-slice_fusion.half_ref), channel_id=1, source_target_pairs={{0,1},{1,0},{2,3},{3,2},{4,5},{5,4},{6,7},{7,6},{8,9},{9,8},{10,11... | collective-permute-start | bytes 3145736 | tf_op jit(solution)/shard_map/ppermute | solution.py:341
  100.1 3.5 %collective-permute-start.20 = (f32[48,512]{1,0:T(8,128)S(1)}, f32[48,512]{1,0:T(8,128)S(1)}, u32[]{:S(2)}, u32[]{:S(2)}) collective-permute-start(f32[48,512]{1,0:T(8,128)S(1)} %maximum_select_fusion), channel_id=1, source_target_pairs={{0,1},{16,17},{32,33},{48,49},{64,65},{80,81},{96,97},{112,113},{1... | collective-permute-start | bytes 294920 | tf_op jit(solution)/shard_map/ppermute | solution.py:351
  103.6 3.5 %collective-permute-start.23 = (f32[48,512]{1,0:T(8,128)S(1)}, f32[48,512]{1,0:T(8,128)S(1)}, u32[]{:S(2)}, u32[]{:S(2)}) collective-permute-start(f32[48,512]{1,0:T(8,128)S(1)} %add.237), channel_id=1, source_target_pairs={{0,4},{1,5},{16,20},{17,21},{32,36},{33,37},{48,52},{49,53},{64,68... | collective-permute-start | bytes 294920 | tf_op jit(solution)/shard_map/ppermute | solution.py:352
  107.2 11.9 %collective-permute-start.24 = (f32[48,512]{1,0:T(8,128)S(1)}, f32[48,512]{1,0:T(8,128)S(1)}, u32[]{:S(2)}, u32[]{:S(2)}) collective-permute-start(f32[48,512]{1,0:T(8,128)S(1)} %add_add_fusion), channel_id=1, source_target_pairs={{0,8},{1,9},{2,10},{3,11},{4,12},{5,13},{6,14},{7,15},{16,24},{17,... | collective-permute-start | bytes 294920 | tf_op jit(solution)/shard_map/ppermute | solution.py:354
  (17 other events, 257.6 us)
Sparse Core Ops, SparseCore 0:
  25.3 46.9 all-gather.2
  97.1 38.9 all-gather.4

commit v2 on v0

--- a/solution.py
+++ b/solution.py
@@ -1,7 +1,20 @@
+import functools
+
 import jax
 import jax.numpy as jnp
 from jax import lax
+from jax.experimental import pallas as pl
+from jax.experimental.pallas import tpu as pltpu
 from jax.sharding import PartitionSpec as P
+
+CAP = 48
+TILE = 512
+LAYERS = 8
+MIB = 1024 * 1024
+VMEM = 60 * MIB
+STAY = 24
+SHARE = 2 * CAP + STAY
+ORDER = (4, 3, 5, 2, 6, 1, 7)
 
 
 def spread(block, axis, holder):
@@ -9,7 +22,7 @@
     return lax.psum(block, axis)
 
 
-def local(matrix, pivot_rows, inv_lower, inv_upper):
+def any_pivots(matrix, pivot_rows, inv_lower, inv_upper):
     best = lax.Precision.HIGHEST
     tiles_down, tile_width, tiles_across, _ = matrix.shape
     row_count = lax.axis_size("row")
@@ -51,6 +64,312 @@
     return result.reshape(tiles_down, tile_width, tiles_across, tile_width)
 
 
+def as_rows(matrix):
+    return matrix.reshape(1024, 2, 4, 128).transpose(0, 2, 1, 3).reshape(1024, 8, 128)
+
+
+def as_matrix(rows):
+    return rows.reshape(1024, 4, 2, 128).transpose(0, 2, 1, 3).reshape(2, 512, 2, 512)
+
+
+def split(value):
+    high = value.astype(jnp.bfloat16)
+    low = (value - high.astype(jnp.float32)).astype(jnp.bfloat16)
+    return high, low
+
+
+def dot3(a_high, a_low, b_high, b_low):
+    dot = functools.partial(jnp.dot, preferred_element_type=jnp.float32)
+    return dot(a_high, b_high) + (dot(a_high, b_low) + dot(a_low, b_high))
+
+
+def whole(memory, count):
+    return [pl.BlockSpec(memory_space=memory)] * count
+
+
+def prepare_kernel(rows_ref, x_ref, first_ref, second_ref, picked_ref, *rest):
+    outs, trades, (x_here, load) = rest[:LAYERS], rest[LAYERS : 2 * LAYERS + 1], rest[2 * LAYERS + 1 :]
+    loads = [
+        pltpu.make_async_copy(x_ref.at[pl.ds(2048 * b, 2048)], x_here.at[pl.ds(2048 * b, 2048)], load.at[b])
+        for b in range(4)
+    ]
+    for copy in loads:
+        copy.start()
+    for b in range(4):
+        loads[b].wait()
+        out_ref = (first_ref, second_ref)[b // 2]
+        for l in range(4):
+            out_ref[256 * (b % 2) : 256 * (b % 2) + 256, 128 * l : 128 * l + 128] = x_here[
+                pl.ds(2048 * b + 2 * l, 256, stride=8), :
+            ]
+
+    def row_of(at):
+        return x_here[pl.ds(pl.multiple_of(rows_ref[at] * 8, 8), 8), :]
+
+    @pl.loop(0, CAP)
+    def _(k):
+        picked_ref[pl.ds(pl.multiple_of(k * 8, 8), 8), :] = row_of(8 + k)
+
+    @pl.when(rows_ref[1] == 0)
+    def _():
+        for k, out in enumerate(outs):
+            for j in range(STAY):
+                out[8 * j : 8 * j + 8, :] = row_of(8 + CAP + STAY * k + j)
+        for k in range(16):
+            out, at = (trades[LAYERS], 8 * CAP * (k // 2)) if k % 2 else (trades[k // 2], 0)
+
+            @pl.loop(0, CAP, unroll=8)
+            def _(j):
+                out[pl.ds(pl.multiple_of(at + 8 * j, 8), 8), :] = row_of(8 + CAP + LAYERS * STAY + CAP * k + j)
+
+
+def prepare(rows, x):
+    half = jax.ShapeDtypeStruct((512, 512), jnp.float32)
+    picked = jax.ShapeDtypeStruct((CAP * 8, 128), jnp.float32)
+    piece = jax.ShapeDtypeStruct((STAY * 8, 128), jnp.float32)
+    group = jax.ShapeDtypeStruct((8 * CAP * LAYERS, 128), jnp.float32)
+    return pl.pallas_call(
+        prepare_kernel,
+        out_shape=[half, half, picked] + [piece] * LAYERS + [picked] * LAYERS + [group],
+        in_specs=whole(pltpu.SMEM, 1) + whole(pl.ANY, 1),
+        out_specs=whole(pltpu.VMEM, 2 * LAYERS + 4),
+        scratch_shapes=[pltpu.VMEM((8192, 128), jnp.float32), pltpu.SemaphoreType.DMA((4,))],
+        compiler_params=pltpu.CompilerParams(vmem_limit_bytes=20 * MIB),
+        cost_estimate=pl.CostEstimate(flops=0, bytes_accessed=10 * MIB, transcendentals=0),
+        name="prepare",
+    )(rows, x)
+
+
+def solve_kernel(rows_ref, half_ref, other_ref, sent_ref, inv_ref, high_ref, low_ref, swapped):
+    core, x = rows_ref[2] % 2, rows_ref[2] // 2 % 4
+    for ref, tile in ((half_ref, core), (other_ref, 1 - core)):
+        for at, size, ahead, skip in ((0, 128, 0, 0), (128, 128, 3, 0), (256, 128, 1, 0), (384, 64, 2, 0), (448, 64, 2, 64)):
+            to = tile * 512 + lax.rem(x + ahead, 4) * 128 + skip
+            swapped[pl.ds(pl.multiple_of(to, 64), size), :] = ref[at : at + size, :]
+
+    @pl.loop(0, rows_ref[0])
+    def _(k):
+        swapped[pl.ds(rows_ref[8 + k], 1), :] = sent_ref[pl.ds(k, 1), :]
+
+    inv_high, inv_low = split(inv_ref[...])
+
+    @pl.loop(0, 4)
+    def _(b):
+        at = pl.ds(pl.multiple_of(b * 256, 256), 256)
+        high, low = split(swapped[at, :])
+        high_ref[at, :], low_ref[at, :] = split(dot3(high, low, inv_high, inv_low))
+
+
+def solve(rows, half, other, sent, inv_upper):
+    part = jax.ShapeDtypeStruct((1024, 512), jnp.bfloat16)
+    return pl.pallas_call(
+        solve_kernel,
+        out_shape=[part, part],
+        in_specs=whole(pltpu.SMEM, 1) + whole(pltpu.VMEM, 4),
+        out_specs=whole(pltpu.VMEM, 2),
+        scratch_shapes=[pltpu.VMEM((1024, 512), jnp.float32)],
+        compiler_params=pltpu.CompilerParams(vmem_limit_bytes=VMEM),
+        cost_estimate=pl.CostEstimate(flops=3 * 2 * 1024 * 512 * 512, bytes_accessed=6 * MIB, transcendentals=0),
+        name="solve",
+    )(rows, half, other, sent, inv_upper)
+
+
+def spread_rows(ref, g_high, g_low):
+    count = ref.shape[0] // 8
+    for sub in range(8):
+        high, low = split(ref[pl.ds(sub, count, stride=8), :])
+        g_high[:, 128 * sub : 128 * sub + 128] = high
+        g_low[:, 128 * sub : 128 * sub + 128] = low
+
+
+def trailing_kernel(
+    rows_ref, x_ref, gathered_all, l_high_all, l_low_all, w_all, new_ref, out_ref,
+    gathered, new_top, l_high, l_low, w_ref, g_high, g_low, u_high, u_low, load,
+):
+    step = pl.program_id(0)
+
+    @pl.when(step == 0)
+    def _():
+        moves = ((gathered_all, gathered), (w_all, w_ref), (l_high_all, l_high), (l_low_all, l_low))
+        copies = [pltpu.make_async_copy(ref, to, load.at[k]) for k, (ref, to) in enumerate(moves)]
+        for copy in copies:
+            copy.start()
+        copies[0].wait()
+
+        @pl.loop(0, TILE, unroll=8)
+        def _(k):
+            at = pl.ds(pl.multiple_of(rows_ref[8 + CAP + k] * 8, 8), 8)
+            new_top[pl.ds(pl.multiple_of(k * 8, 8), 8), :] = gathered[at, :]
+
+        spread_rows(new_top, g_high, g_low)
+        copies[1].wait()
+        w_high, w_low = split(w_ref[...])
+        for n in range(4):
+            at = slice(256 * n, 256 * n + 256)
+            u_high[:, at], u_low[:, at] = split(dot3(w_high, w_low, g_high[:, at], g_low[:, at]))
+        copies[2].wait()
+        copies[3].wait()
+
+    @pl.when(step > 0)
+    def _():
+        block = step - 1
+        out_ref[...] = x_ref[...]
+
+        @pl.loop(rows_ref[2 + step], rows_ref[3 + step])
+        def _(k):
+            to = pl.ds(pl.multiple_of((rows_ref[8 + k] - block * 256) * 8, 8), 8)
+            out_ref[to, :] = new_ref[pl.ds(pl.multiple_of(k * 8, 8), 8), :]
+
+        here = pl.ds(pl.multiple_of(block * 256, 256), 256)
+        high, low = l_high[here, :], l_low[here, :]
+        for n in range(4):
+            at = slice(256 * n, 256 * n + 256)
+            product = dot3(high, low, u_high[:, at], u_low[:, at])
+            for part in range(2):
+                to = pl.ds(2 * n + part, 256, stride=8)
+                out_ref[to, :] = out_ref[to, :] - product[:, 128 * part : 128 * part + 128]
+
+        @pl.when(rows_ref[2] == 0)
+        def _():
+            lower = high.astype(jnp.float32) + low.astype(jnp.float32)
+            for l in range(4):
+                out_ref[pl.ds(2 * l, 256, stride=8), :] = lower[:, 128 * l : 128 * l + 128]
+
+        @pl.when((rows_ref[1] == 0) & (block < 2))
+        def _():
+            at = pl.ds(pl.multiple_of(lax.rem(block, 2) * 256, 256), 256)
+            for sub in range(8):
+                cols = slice(128 * sub, 128 * sub + 128)
+                u = u_high[at, cols].astype(jnp.float32) + u_low[at, cols].astype(jnp.float32)
+                out_ref[pl.ds(sub, 256, stride=8), :] = u
+
+
+def trailing(rows, x, gathered, l_high, l_low, weights, new):
+    block = pl.BlockSpec((2048, 128), lambda i, *_: (jnp.maximum(i - 1, 0), 0))
+    return pl.pallas_call(
+        trailing_kernel,
+        out_shape=jax.ShapeDtypeStruct((8192, 128), jnp.float32),
+        grid_spec=pltpu.PrefetchScalarGridSpec(
+            num_scalar_prefetch=1,
+            grid=(5,),
+            in_specs=[block] + whole(pl.ANY, 4) + whole(pltpu.VMEM, 1),
+            out_specs=block,
+            scratch_shapes=[pltpu.VMEM((8 * LAYERS * SHARE, 128), jnp.float32), pltpu.VMEM((4096, 128), jnp.float32)]
+            + [pltpu.VMEM((1024, 512), jnp.bfloat16)] * 2
+            + [pltpu.VMEM((512, 512), jnp.float32)]
+            + [pltpu.VMEM((512, 1024), jnp.bfloat16)] * 4
+            + [pltpu.SemaphoreType.DMA((4,))],
+        ),
+        compiler_params=pltpu.CompilerParams(vmem_limit_bytes=VMEM),
+        cost_estimate=pl.CostEstimate(flops=3 * 2 * 1024 * 512 * 1536, bytes_accessed=18 * MIB, transcendentals=0),
+        name="trailing",
+    )(rows, x, gathered, l_high, l_low, weights, new)
+
+
+def x_shift(value, by):
+    return lax.ppermute(value, "col", [(i, i // 8 * 8 + (i // 2 + by) % 4 * 2 + i % 2) for i in range(16)])
+
+
+def swap(value, axis):
+    return lax.ppermute(value, axis, [(i, i ^ 1) for i in range(16)])
+
+
+def gather_layers(piece):
+    groups = [[2 * i + j for i in range(LAYERS)] for j in range(2)]
+    return lax.all_gather(piece, "row", axis_index_groups=groups, axis=0, tiled=True)
+
+
+def scatter_panel(first, second, col):
+    core, x = col % 2, col // 2 % 4
+    half = jnp.where(core == 0, first, lax.ppermute(second, "col", [(0, 1)]))
+    mine = jnp.where(x == 0, half[:128], 0.0)
+    got = [
+        lax.ppermute(half[128 * to : 128 * to + 128], "col", [(0, 2 * to), (1, 2 * to + 1)])
+        for to in (1, 3, 2)
+    ]
+    return jnp.where(col < 8, mine + got[0] + got[1] + got[2], 0.0)
+
+
+def gather_panel(mine):
+    mine = mine + lax.ppermute(mine, "col", [(i, i + 8) for i in range(8)])
+    up, down = x_shift(mine, 1), x_shift(mine, -1)
+    half = jnp.concatenate([mine, up, down, x_shift(up[:64], 1), x_shift(down[64:], -1)])
+    return half, swap(half, "col")
+
+
+def across(value, col):
+    value = jnp.where(col == 0, value, 0.0)
+    value = value + lax.ppermute(value, "col", [(0, 1)])
+    got = [lax.ppermute(value, "col", [(0, 2 * to), (1, 2 * to + 1)]) for to in (1, 3, 2)]
+    value = value + got[0] + got[1] + got[2]
+    return value + lax.ppermute(value, "col", [(i, i + 8) for i in range(8)])
+
+
+def few_pivots(matrix, pivot_rows, inv_lower, inv_upper, owner, rank):
+    row, col = lax.axis_index("row"), lax.axis_index("col")
+    y = row % 2
+    x2 = as_rows(matrix).reshape(8192, 128)
+
+    index = jnp.arange(TILE, dtype=jnp.int32)
+    here = pivot_rows // TILE // 16 * TILE + pivot_rows % TILE
+    capped = jnp.minimum(rank, jnp.where(owner < 0, LAYERS * STAY, CAP) - 1)
+    key = jnp.where(owner < 0, -1, owner * CAP + capped)
+
+    def listed(keys, values, count, first=0):
+        slots = jnp.arange(count, dtype=jnp.int32) + first
+        return jnp.sum(jnp.where(keys[:, None] == slots[None, :], values[:, None], 0), axis=0)
+
+    at_rows = jnp.minimum(listed(key - row * CAP, here, CAP), 1023)
+    staying = jnp.minimum(listed(jnp.where(owner < 0, capped, -1), index, LAYERS * STAY), TILE - 1)
+    going = jnp.minimum(listed(key, index, 16 * CAP), TILE - 1)
+    moved_at = owner // 2 * SHARE + owner % 2 * CAP + capped
+    stay_at = capped // STAY * SHARE + 2 * CAP + capped % STAY
+    lies_at = jnp.where(owner < 0, stay_at, moved_at)
+    limits = 256 * jnp.arange(5, dtype=jnp.int32)
+    below = jnp.sum(((owner == row)[None] & (here[None] < limits[:, None])).astype(jnp.int32), axis=1)
+    below = jnp.minimum(below, CAP)
+    place = jnp.stack([row, col]).astype(jnp.int32)
+    rows = jnp.concatenate([below[4:], place, below, at_rows, lies_at])
+    head = jnp.concatenate([jnp.zeros(1, jnp.int32), place, jnp.zeros(5, jnp.int32)])
+    first, second, picked, *sends = prepare(jnp.concatenate([head, at_rows, staying, going]), x2)
+    share, packed = sends[:LAYERS], sends[LAYERS:]
+
+    odd = lax.ppermute(packed[LAYERS], "row", [(0, 1)])
+    pieces = [jnp.where(row == 0, packed[k], odd[8 * CAP * k : 8 * CAP * (k + 1)]) for k in range(LAYERS)]
+    new = jnp.where(row < 2, pieces[0], 0.0)
+    for to in ORDER:
+        new = new + lax.ppermute(pieces[to], "row", [(0, 2 * to), (1, 2 * to + 1)])
+
+    paired = swap(picked, "row")
+    piece = jnp.where(row == 0, share[0], 0.0)
+    for to in ORDER:
+        piece = piece + lax.ppermute(share[to], "row", [(0, 2 * to)])
+    piece = piece + lax.ppermute(piece, "row", [(2 * i, 2 * i + 1) for i in range(LAYERS)])
+    gathered = gather_layers(
+        jnp.concatenate([jnp.where(y == 0, picked, paired), jnp.where(y == 0, paired, picked), piece])
+    )
+
+    half, other_half = gather_panel(scatter_panel(first, second, col))
+    sent = across(new.reshape(CAP, 4, 2, 128)[:, :, 0].reshape(CAP, TILE), col)
+    l_high, l_low = solve(rows, half, other_half, sent, inv_upper)
+    out = trailing(rows, x2, gathered, l_high, l_low, inv_lower, new)
+    return as_matrix(out.reshape(1024, 8, 128))
+
+
+def local(matrix, pivot_rows, inv_lower, inv_upper):
+    moved = pivot_rows >= TILE
+    owner = jnp.where(moved, pivot_rows // TILE % 16, -1)
+    before = (owner[:, None] == owner[None, :]) & (pivot_rows[None, :] < pivot_rows[:, None])
+    rank = jnp.sum(before.astype(jnp.int32), axis=1)
+    crowded = jnp.any(rank >= jnp.where(moved, CAP, LAYERS * STAY))
+    out = few_pivots(matrix, pivot_rows, inv_lower, inv_upper, owner, rank)
+
+    def body(state):
+        return jnp.bool_(False), any_pivots(matrix, pivot_rows, inv_lower, inv_upper)
+
+    return lax.while_loop(lambda state: state[0], body, (crowded, out))[1]
+
+
 def solution(mesh):
     return jax.shard_map(
         local,

time: 421 us -> 168 us (0.40); the launches traced: 415 us -> 167 us
  waiting for transfers between devices: 339 us -> 79.1 us
  starting transfers between devices: 0.22 us -> 29.3 us
  Pallas kernels: 0 us -> 23.4 us
  matrix products: 19.6 us -> 0 us
  local copies, waits for them, and re-layouts: 27.9 us -> 9.24 us
    psum x2 -> x0, waiting for transfers between devices: 339 us -> none  [spread(): return lax.psum(block, axis)]
    ppermute x0 -> x32, waiting for transfers between devices: none -> 79.1 us  [the longest x7 33.1 us: few_pivots(): new = new + lax.ppermute(pieces[to], 'row', [(0, 2 * to), (1, 2 * to + 1)])]
    ppermute x0 -> x32, starting transfers between devices: none -> 29.3 us  [the longest x7 7.14 us: few_pivots(): piece = piece + lax.ppermute(share[to], 'row', [(0, 2 * to)])]
    pallas_call x0 -> x3, Pallas kernels: none -> 23.4 us  [the longest x1 14.2 us: trailing(): pl.pallas_call(trailing_kernel, out_shape=jax.ShapeDtypeStruct((8192, 128...]
    dot_general x3 -> x0, matrix products: 19.6 us -> none  [the longest x1 9.52 us: local(): jnp.dot(lower_cols, upper_rows, precision=best, preferred_element_type=jn...]
    gather x2 -> x0, local copies, waits for them, and re-layouts: 13 us -> none  [the longest x1 7.95 us: local(): swapped = jnp.where(has_source[:, None], former_top[source], matrix_here)]
    reshape x1 -> x0, local copies, waits for them, and re-layouts: 6.57 us -> none  [local(): return result.reshape(tiles_down, tile_width, tiles_across, tile_width)]
    select_n x6, other arithmetic: 9.14 us -> 3.83 us  [the longest x1 1.55 us: few_pivots(): jnp.where(row == 0, packed[k], odd[8 * CAP * k:8 * CAP * (k + 1)])]
  transfers between devices with their start and end apart: 2 -> 33, of which waited for: 2 -> 7; matrix products, arithmetic and copies ran while one was open for 2% -> 7% of each run, Pallas kernels for 0% -> 4%
where the time goes in v2:
time: 168 us; the launch traced here: 167 us
  waiting for transfers between devices  79.1 us (47%)
  starting transfers between devices  29.3 us (17%)
  Pallas kernels  23.4 us (14%)
  between operations  13.9 us (8%)
  other arithmetic  11.6 us (7%)
  local copies, waits for them, and re-layouts  9.24 us (6%)
    ppermute x7, waiting for transfers between devices, few_pivots(): new = new + lax.ppermute(pieces[to], 'row', [(0, 2 * to), (1, 2 * to + 1)])  33.1 us
    ppermute x1, waiting for transfers between devices, across(): return value + lax.ppermute(value, 'col', [(i, i + 8) for i in range(8)])  14.7 us
    pallas_call x1, Pallas kernels, trailing(): pl.pallas_call(trailing_kernel, out_shape=jax.ShapeDtypeStruct((8192, 128...  14.2 us
    ppermute x1, waiting for transfers between devices, few_pivots(): lax.ppermute(piece, 'row', [(2 * i, 2 * i + 1) for i in range(LAYERS)])  13.7 us
    ppermute x1, waiting for transfers between devices, gather_panel(): mine = mine + lax.ppermute(mine, 'col', [(i, i + 8) for i in range(8)])  10.1 us
    ppermute x4, waiting for transfers between devices, x_shift(): lax.ppermute(value, 'col', [(i, i // 8 * 8 + (i // 2 + by) % 4 * 2 + i %...  7.43 us
    ppermute x7, starting transfers between devices, few_pivots(): piece = piece + lax.ppermute(share[to], 'row', [(0, 2 * to)])  7.14 us
    unnamed x24, local copies, waits for them, and re-layouts  6.5 us
  transfers between devices with their start and end apart: 33, of which 7 were waited for; matrix products, arithmetic and copies ran while one was open for 7% of the time, Pallas kernels for 4%

profile of v2, /device:TPU:58, one launch (start us, length us, event | category | flops | bytes accessed | tf_op | source)
XLA Modules:
  0.0 167.2 jit_solution(16228733521727734751)
XLA Ops:
  9.6 3.2 %prepare.1 = (f32[512,512]{1,0:T(8,128)S(1)}, f32[512,512]{1,0:T(8,128)S(1)}, f32[384,128]{1,0:T(8,128)S(1)}, f32[192,128]{1,0:T(8,128)S(1)}, f32[192,128]{1,0:T...) custom-call(s32[1016]{0:T(1024)S(1)} %concatenate.21.rows_ref, ...), custom_call_target="tpu_custom_call" | custom-call | bytes 10485760 | tf_op jit(solution)/shard_map/prepare/pallas_call | solution.py:131
  17.0 1.3 collective-permute-start.4
  18.3 1.3 collective-permute-start.5
  19.6 1.3 collective-permute-start.6
  21.5 1.3 collective-permute-start.7
  24.2 1.2 add_add_fusion.1
  25.5 1.3 collective-permute-start.8
  26.8 13.7 %collective-permute-done.8 = f32[192,128]{1,0:T(8,128)S(1)} collective-permute-done((f32[192,128]{1,0:T(8,128)S(1)}, f32[192,128]{1,0:T(8,128)S(1)}, u32[]{:S(2)}, u32[]{:S(2)}) %collective-permute-start.8) | collective-permute-done | bytes 98336 | tf_op jit(solution)/shard_map/ppermute | solution.py:347
  41.4 1.6 collective-permute-start.9
  43.1 1.9 %collective-permute-start.19 = (f32[3072,128]{1,0:T(8,128)}, f32[3072,128]{1,0:T(8,128)}, u32[]{:S(2)}, u32[]{:S(2)}) collective-permute-start(f32[3072,128]{1,0:T(8,128)} %copy-done), channel_id=1, source_target_pairs={{0,16},{1,17},{2,18},{3,19},{4,20},{5,21},{6,22},{7,23},{8,24},{9,... | collective-permute-start | bytes 4718600 | tf_op jit(solution)/shard_map/ppermute | solution.py:337
  49.4 1.3 collective-permute-start.13
  50.7 1.5 slice_select_fusion.9
  53.6 1.3 collective-permute-start.25
  55.6 10.1 %collective-permute-done.13 = f32[128,512]{1,0:T(8,128)S(1)} collective-permute-done((f32[128,512]{1,0:T(8,128)S(1)}, f32[128,512]{1,0:T(8,128)S(1)}, u32[]{:S(2)}, u32[]{:S(2)}) %collective-permute-start.13) | collective-permute-done | bytes 262176 | tf_op jit(solution)/shard_map/ppermute | solution.py:294
  68.5 33.1 %collective-permute-done.25 = f32[384,128]{1,0:T(8,128)S(1)} collective-permute-done((f32[384,128]{1,0:T(8,128)S(1)}, f32[384,128]{1,0:T(8,128)S(1)}, u32[]{:S(2)}, u32[]{:S(2)}) %collective-permute-start.25) | collective-permute-done | bytes 196640 | tf_op jit(solution)/shard_map/ppermute | solution.py:341
  102.1 1.5 collective-permute-start.14
  104.7 4.0 %collective-permute-done.15 = f32[128,512]{1,0:T(8,128)S(1)} collective-permute-done((f32[128,512]{1,0:T(8,128)S(1)}, f32[128,512]{1,0:T(8,128)S(1)}, u32[]{:S(2)}, u32[]{:S(2)}) %collective-permute-start.15) | collective-permute-done | bytes 262176 | tf_op jit(solution)/shard_map/ppermute | solution.py:270
  109.2 1.8 %collective-permute-start.16 = (f32[64,512]{1,0:T(8,128)S(1)}, f32[64,512]{1,0:T(8,128)S(1)}, u32[]{:S(2)}, u32[]{:S(2)}) collective-permute-start(f32[64,512]{1,0:T(8,128)S(1)} %slice.96), channel_id=1, source_target_pairs={{0,2},{1,3},{2,4},{3,5},{4,6},{5,7},{6,0},{7,1},{8,10},{9,11},{10,... | collective-permute-start | bytes 393224 | tf_op jit(solution)/shard_map/ppermute | solution.py:270
  112.4 3.1 %collective-permute-done.16 = f32[64,512]{1,0:T(8,128)S(1)} collective-permute-done((f32[64,512]{1,0:T(8,128)S(1)}, f32[64,512]{1,0:T(8,128)S(1)}, u32[]{:S(2)}, u32[]{:S(2)}) %collective-permute-start.16) | collective-permute-done | bytes 131104 | tf_op jit(solution)/shard_map/ppermute | solution.py:270
  120.7 1.3 concatenate.20.rows_ref
  122.1 1.3 collective-permute-start.31
  124.1 14.7 %collective-permute-done.31 = f32[48,512]{1,0:T(8,128)S(1)} collective-permute-done((f32[48,512]{1,0:T(8,128)S(1)}, f32[48,512]{1,0:T(8,128)S(1)}, u32[]{:S(2)}, u32[]{:S(2)}) %collective-permute-start.31) | collective-permute-done | bytes 98336 | tf_op jit(solution)/shard_map/ppermute | solution.py:305
  139.5 6.0 %solve.1 = (bf16[1024,512]{1,0:T(8,128)(2,1)}, bf16[1024,512]{1,0:T(8,128)(2,1)}) custom-call(s32[568]{0:T(1024)} %concatenate.20.rows_ref, f32[512,512]{1,0:T(8,128)} %constant_dynamic-update-slice_fusion.half_ref, f32[512,512]{1,0:T(8,128)} %collective-permute-done.18.other_ref, f32[48,512]{1,0:T(8,128)} %add.292.sent_ref, f32[512,512]{1,0:T(8,128)S(1)} %copy-done.6), custom_call_target="tpu_custom_call" | custom-call | flops 1610612736 | bytes 6291456 | tf_op jit(solution)/shard_map/solve/pallas_call | solution.py:165
  145.5 14.2 %trailing.1 = f32[8192,128]{1,0:T(8,128)} custom-call(s32[568]{0:T(1024)} %concatenate.20.rows_ref, f32[8192,128]{1,0:T(8,128)} %bitcast.39, f32[7680,128]{1,0:T(8,128)} %all-gather.2.cloned.1.call-done.gathered_all, bf16[1024,512]{1,0:T(8,128)(2,1)} %get-tuple-element.77.l_high_all, bf16[1024,512]{1,0:T(8,128)(2,1)} %get-tuple-element.78.l_low_all, ...), custom_call_target="tpu_custom_call" | custom-call | flops 4831838208 | bytes 18874368 | tf_op jit(solution)/shard_map/trailing/pallas_call | solution.py:249
  (105 shorter events, 30.0 us)
Async XLA Ops:
  6.5 138.9 %all-gather.2.cloned.1.call-start = ((), (), s32[]{:S(2)}) async-start(), calls=%async_computation.2 | async-start | bytes 4423680 | tf_op jit(solution)/shard_map/all_gather | solution.py:279
  15.0 4.6 %collective-permute-start.1 = (f32[192,128]{1,0:T(8,128)S(1)}, f32[192,128]{1,0:T(8,128)S(1)}, u32[]{:S(2)}, u32[]{:S(2)}) collective-permute-start(f32[192,128]{1,0:T(8,128)S(1)} %get-tuple-element.59), channel_id=1, source_target_pairs={{0,128},{1,129},{2,130},{3,131},{4,132},{5,133},{6,134},{7,135},{8... | collective-permute-start | bytes 294920 | tf_op jit(solution)/shard_map/ppermute | solution.py:346
  15.7 5.2 %collective-permute-start.2 = (f32[192,128]{1,0:T(8,128)S(1)}, f32[192,128]{1,0:T(8,128)S(1)}, u32[]{:S(2)}, u32[]{:S(2)}) collective-permute-start(f32[192,128]{1,0:T(8,128)S(1)} %get-tuple-element.60), channel_id=1, source_target_pairs={{0,96},{1,97},{2,98},{3,99},{4,100},{5,101},{6,102},{7,103},{8,104... | collective-permute-start | bytes 294920 | tf_op jit(solution)/shard_map/ppermute | solution.py:346
  16.3 6.5 %collective-permute-start.3 = (f32[192,128]{1,0:T(8,128)S(1)}, f32[192,128]{1,0:T(8,128)S(1)}, u32[]{:S(2)}, u32[]{:S(2)}) collective-permute-start(f32[192,128]{1,0:T(8,128)S(1)} %get-tuple-element.61), channel_id=1, source_target_pairs={{0,160},{1,161},{2,162},{3,163},{4,164},{5,165},{6,166},{7,167},{8... | collective-permute-start | bytes 294920 | tf_op jit(solution)/shard_map/ppermute | solution.py:346
  17.0 7.2 %collective-permute-start.4 = (f32[192,128]{1,0:T(8,128)S(1)}, f32[192,128]{1,0:T(8,128)}, u32[]{:S(2)}, u32[]{:S(2)}) collective-permute-start(f32[192,128]{1,0:T(8,128)S(1)} %get-tuple-element.62), channel_id=1, source_target_pairs={{0,64},{1,65},{2,66},{3,67},{4,68},{5,69},{6,70},{7,71},{8,72},{9,... | collective-permute-start | bytes 294920 | tf_op jit(solution)/shard_map/ppermute | solution.py:346
  18.3 5.9 %collective-permute-start.5 = (f32[192,128]{1,0:T(8,128)S(1)}, f32[192,128]{1,0:T(8,128)}, u32[]{:S(2)}, u32[]{:S(2)}) collective-permute-start(f32[192,128]{1,0:T(8,128)S(1)} %get-tuple-element.63), channel_id=1, source_target_pairs={{0,192},{1,193},{2,194},{3,195},{4,196},{5,197},{6,198},{7,199},{8... | collective-permute-start | bytes 294920 | tf_op jit(solution)/shard_map/ppermute | solution.py:346
  19.6 4.6 %collective-permute-start.6 = (f32[192,128]{1,0:T(8,128)S(1)}, f32[192,128]{1,0:T(8,128)}, u32[]{:S(2)}, u32[]{:S(2)}) collective-permute-start(f32[192,128]{1,0:T(8,128)S(1)} %get-tuple-element.64), channel_id=1, source_target_pairs={{0,32},{1,33},{2,34},{3,35},{4,36},{5,37},{6,38},{7,39},{8,40},{9,... | collective-permute-start | bytes 294920 | tf_op jit(solution)/shard_map/ppermute | solution.py:346
  23.5 17.0 %collective-permute-start = (f32[384,128]{1,0:T(8,128)S(1)}, f32[384,128]{1,0:T(8,128)S(1)}, u32[]{:S(2)}, u32[]{:S(2)}) collective-permute-start(f32[384,128]{1,0:T(8,128)S(1)} %get-tuple-element.57), channel_id=1, source_target_pairs={{0,16},{16,0},{32,48},{48,32},{64,80},{80,64},{96,112},{112,96},{1... | collective-permute-start | bytes 589832 | tf_op jit(solution)/shard_map/ppermute | solution.py:274
  25.5 15.0 %collective-permute-start.8 = (f32[192,128]{1,0:T(8,128)S(1)}, f32[192,128]{1,0:T(8,128)S(1)}, u32[]{:S(2)}, u32[]{:S(2)}) collective-permute-start(f32[192,128]{1,0:T(8,128)S(1)} %add_add_fusion.1), channel_id=1, source_target_pairs={{0,16},{32,48},{64,80},{96,112},{128,144},{160,176},{192,208},{224... | collective-permute-start | bytes 294920 | tf_op jit(solution)/shard_map/ppermute | solution.py:347
  43.1 7.6 %collective-permute-start.19 = (f32[3072,128]{1,0:T(8,128)}, f32[3072,128]{1,0:T(8,128)}, u32[]{:S(2)}, u32[]{:S(2)}) collective-permute-start(f32[3072,128]{1,0:T(8,128)} %copy-done), channel_id=1, source_target_pairs={{0,16},{1,17},{2,18},{3,19},{4,20},{5,21},{6,22},{7,23},{8,24},{9,... | collective-permute-start | bytes 4718600 | tf_op jit(solution)/shard_map/ppermute | solution.py:337
  49.4 16.3 %collective-permute-start.13 = (f32[128,512]{1,0:T(8,128)S(1)}, f32[128,512]{1,0:T(8,128)S(1)}, u32[]{:S(2)}, u32[]{:S(2)}) collective-permute-start(f32[128,512]{1,0:T(8,128)S(1)} %fusion.29), channel_id=1, source_target_pairs={{0,8},{1,9},{2,10},{3,11},{4,12},{5,13},{6,14},{7,15},{16,24},{17,... | collective-permute-start | bytes 786440 | tf_op jit(solution)/shard_map/ppermute | solution.py:294
  52.2 14.1 %collective-permute-start.20 = (f32[384,128]{1,0:T(8,128)S(1)}, f32[384,128]{1,0:T(8,128)S(1)}, u32[]{:S(2)}, u32[]{:S(2)}) collective-permute-start(f32[384,128]{1,0:T(8,128)S(1)} %get-tuple-element.103), channel_id=1, source_target_pairs={{0,128},{16,144},{1,129},{17,145},{2,130},{18,146},{3,131},{19,147... | collective-permute-start | bytes 589832 | tf_op jit(solution)/shard_map/ppermute | solution.py:341
  52.9 14.1 %collective-permute-start.26 = (f32[384,128]{1,0:T(8,128)S(1)}, f32[384,128]{1,0:T(8,128)S(1)}, u32[]{:S(2)}, u32[]{:S(2)}) collective-permute-start(f32[384,128]{1,0:T(8,128)S(1)} %get-tuple-element.104), channel_id=1, source_target_pairs={{0,224},{16,240},{1,225},{17,241},{2,226},{18,242},{3,227},{19,243... | collective-permute-start | bytes 589832 | tf_op jit(solution)/shard_map/ppermute | solution.py:341
  53.6 48.0 %collective-permute-start.25 = (f32[384,128]{1,0:T(8,128)S(1)}, f32[384,128]{1,0:T(8,128)S(1)}, u32[]{:S(2)}, u32[]{:S(2)}) collective-permute-start(f32[384,128]{1,0:T(8,128)S(1)} %get-tuple-element.105), channel_id=1, source_target_pairs={{0,32},{16,48},{1,33},{17,49},{2,34},{18,50},{3,35},{19,51},{4,36}... | collective-permute-start | bytes 589832 | tf_op jit(solution)/shard_map/ppermute | solution.py:341
  54.9 47.2 %collective-permute-start.24 = (f32[384,128]{1,0:T(8,128)S(1)}, f32[384,128]{1,0:T(8,128)S(1)}, u32[]{:S(2)}, u32[]{:S(2)}) collective-permute-start(f32[384,128]{1,0:T(8,128)S(1)} %get-tuple-element.106), channel_id=1, source_target_pairs={{0,192},{16,208},{1,193},{17,209},{2,194},{18,210},{3,195},{19,211... | collective-permute-start | bytes 589832 | tf_op jit(solution)/shard_map/ppermute | solution.py:341
  65.7 37.9 %collective-permute-start.23 = (f32[384,128]{1,0:T(8,128)S(1)}, f32[384,128]{1,0:T(8,128)S(1)}, u32[]{:S(2)}, u32[]{:S(2)}) collective-permute-start(f32[384,128]{1,0:T(8,128)S(1)} %get-tuple-element.107), channel_id=1, source_target_pairs={{0,64},{16,80},{1,65},{17,81},{2,66},{18,82},{3,67},{19,83},{4,68}... | collective-permute-start | bytes 589832 | tf_op jit(solution)/shard_map/ppermute | solution.py:341
  66.3 37.3 %collective-permute-start.22 = (f32[384,128]{1,0:T(8,128)S(1)}, f32[384,128]{1,0:T(8,128)S(1)}, u32[]{:S(2)}, u32[]{:S(2)}) collective-permute-start(f32[384,128]{1,0:T(8,128)S(1)} %get-tuple-element.108), channel_id=1, source_target_pairs={{0,160},{16,176},{1,161},{17,177},{2,162},{18,178},{3,163},{19,179... | collective-permute-start | bytes 589832 | tf_op jit(solution)/shard_map/ppermute | solution.py:341
  67.0 36.6 %collective-permute-start.21 = (f32[384,128]{1,0:T(8,128)S(1)}, f32[384,128]{1,0:T(8,128)S(1)}, u32[]{:S(2)}, u32[]{:S(2)}) collective-permute-start(f32[384,128]{1,0:T(8,128)S(1)} %get-tuple-element.109), channel_id=1, source_target_pairs={{0,96},{16,112},{1,97},{17,113},{2,98},{18,114},{3,99},{19,115},{4... | collective-permute-start | bytes 589832 | tf_op jit(solution)/shard_map/ppermute | solution.py:341
  101.6 7.1 %collective-permute-start.15 = (f32[128,512]{1,0:T(8,128)S(1)}, f32[128,512]{1,0:T(8,128)S(1)}, u32[]{:S(2)}, u32[]{:S(2)}) collective-permute-start(f32[128,512]{1,0:T(8,128)S(1)} %get-tuple-element.95), channel_id=1, source_target_pairs={{0,6},{1,7},{2,0},{3,1},{4,2},{5,3},{6,4},{7,5},{8,14},{9,15},{10,... | collective-permute-start | bytes 786440 | tf_op jit(solution)/shard_map/ppermute | solution.py:270
  102.1 7.0 %collective-permute-start.14 = (f32[128,512]{1,0:T(8,128)S(1)}, f32[128,512]{1,0:T(8,128)S(1)}, u32[]{:S(2)}, u32[]{:S(2)}) collective-permute-start(f32[128,512]{1,0:T(8,128)S(1)} %get-tuple-element.95), channel_id=1, source_target_pairs={{0,2},{1,3},{2,4},{3,5},{4,6},{5,7},{6,0},{7,1},{8,10},{9,11},{10,... | collective-permute-start | bytes 786440 | tf_op jit(solution)/shard_map/ppermute | solution.py:270
  108.7 7.5 %collective-permute-start.17 = (f32[64,512]{1,0:T(8,128)S(1)}, f32[64,512]{1,0:T(8,128)S(1)}, u32[]{:S(2)}, u32[]{:S(2)}) collective-permute-start(f32[64,512]{1,0:T(8,128)S(1)} %slice.97), channel_id=1, source_target_pairs={{0,6},{1,7},{2,0},{3,1},{4,2},{5,3},{6,4},{7,5},{8,14},{9,15},{10,... | collective-permute-start | bytes 393224 | tf_op jit(solution)/shard_map/ppermute | solution.py:270
  109.2 6.3 %collective-permute-start.16 = (f32[64,512]{1,0:T(8,128)S(1)}, f32[64,512]{1,0:T(8,128)S(1)}, u32[]{:S(2)}, u32[]{:S(2)}) collective-permute-start(f32[64,512]{1,0:T(8,128)S(1)} %slice.96), channel_id=1, source_target_pairs={{0,2},{1,3},{2,4},{3,5},{4,6},{5,7},{6,0},{7,1},{8,10},{9,11},{10,... | collective-permute-start | bytes 393224 | tf_op jit(solution)/shard_map/ppermute | solution.py:270
  116.9 22.6 %collective-permute-start.18 = (f32[512,512]{1,0:T(8,128)}, f32[512,512]{1,0:T(8,128)}, u32[]{:S(2)}, u32[]{:S(2)}) collective-permute-start(f32[512,512]{1,0:T(8,128)} %constant_dynamic-update-slice_fusion.half_ref), channel_id=1, source_target_pairs={{0,1},{1,0},{2,3},{3,2},{4,5},{5,4},{6,7},{7,6},{8,9},{9,8},{10,11... | collective-permute-start | bytes 3145736 | tf_op jit(solution)/shard_map/ppermute | solution.py:274
  122.1 16.7 %collective-permute-start.31 = (f32[48,512]{1,0:T(8,128)S(1)}, f32[48,512]{1,0:T(8,128)S(1)}, u32[]{:S(2)}, u32[]{:S(2)}) collective-permute-start(f32[48,512]{1,0:T(8,128)S(1)} %add_add_fusion), channel_id=1, source_target_pairs={{0,8},{1,9},{2,10},{3,11},{4,12},{5,13},{6,14},{7,15},{16,24},{17,... | collective-permute-start | bytes 294920 | tf_op jit(solution)/shard_map/ppermute | solution.py:305
  (19 other events, 122.8 us)
Sparse Core Ops, SparseCore 0:
  41.6 57.9 all-gather.1

commit v3 on v2

--- a/solution.py
+++ b/solution.py
@@ -88,7 +88,7 @@
 
 
 def prepare_kernel(rows_ref, x_ref, first_ref, second_ref, picked_ref, *rest):
-    outs, trades, (x_here, load) = rest[:LAYERS], rest[LAYERS : 2 * LAYERS + 1], rest[2 * LAYERS + 1 :]
+    outs, (x_here, load) = rest[:LAYERS], rest[LAYERS:]
     loads = [
         pltpu.make_async_copy(x_ref.at[pl.ds(2048 * b, 2048)], x_here.at[pl.ds(2048 * b, 2048)], load.at[b])
         for b in range(4)
@@ -115,28 +115,53 @@
         for k, out in enumerate(outs):
             for j in range(STAY):
                 out[8 * j : 8 * j + 8, :] = row_of(8 + CAP + STAY * k + j)
-        for k in range(16):
-            out, at = (trades[LAYERS], 8 * CAP * (k // 2)) if k % 2 else (trades[k // 2], 0)
-
-            @pl.loop(0, CAP, unroll=8)
-            def _(j):
-                out[pl.ds(pl.multiple_of(at + 8 * j, 8), 8), :] = row_of(8 + CAP + LAYERS * STAY + CAP * k + j)
 
 
 def prepare(rows, x):
     half = jax.ShapeDtypeStruct((512, 512), jnp.float32)
     picked = jax.ShapeDtypeStruct((CAP * 8, 128), jnp.float32)
     piece = jax.ShapeDtypeStruct((STAY * 8, 128), jnp.float32)
-    group = jax.ShapeDtypeStruct((8 * CAP * LAYERS, 128), jnp.float32)
     return pl.pallas_call(
         prepare_kernel,
-        out_shape=[half, half, picked] + [piece] * LAYERS + [picked] * LAYERS + [group],
+        out_shape=[half, half, picked] + [piece] * LAYERS,
         in_specs=whole(pltpu.SMEM, 1) + whole(pl.ANY, 1),
-        out_specs=whole(pltpu.VMEM, 2 * LAYERS + 4),
+        out_specs=whole(pltpu.VMEM, LAYERS + 3),
         scratch_shapes=[pltpu.VMEM((8192, 128), jnp.float32), pltpu.SemaphoreType.DMA((4,))],
         compiler_params=pltpu.CompilerParams(vmem_limit_bytes=20 * MIB),
         cost_estimate=pl.CostEstimate(flops=0, bytes_accessed=10 * MIB, transcendentals=0),
         name="prepare",
+    )(rows, x)
+
+
+def pack_kernel(rows_ref, x_ref, *rest):
+    outs, (x_here, load) = rest[: LAYERS + 1], rest[LAYERS + 1 :]
+
+    @pl.when(rows_ref[0] == 0)
+    def _():
+        copy = pltpu.make_async_copy(x_ref.at[pl.ds(0, 4096)], x_here, load)
+        copy.start()
+        copy.wait()
+        places = [(outs[LAYERS], 8 * CAP * (k // 2)) if k % 2 else (outs[k // 2], 0) for k in range(16)]
+        for k, (out, at) in enumerate(places):
+
+            @pl.loop(0, CAP, unroll=8)
+            def _(j):
+                to = pl.ds(pl.multiple_of(at + 8 * j, 8), 8)
+                out[to, :] = x_here[pl.ds(pl.multiple_of(rows_ref[8 + CAP * k + j] * 8, 8), 8), :]
+
+
+def pack(rows, x):
+    piece = jax.ShapeDtypeStruct((8 * CAP, 128), jnp.float32)
+    group = jax.ShapeDtypeStruct((8 * CAP * LAYERS, 128), jnp.float32)
+    return pl.pallas_call(
+        pack_kernel,
+        out_shape=[piece] * LAYERS + [group],
+        in_specs=whole(pltpu.SMEM, 1) + whole(pl.ANY, 1),
+        out_specs=whole(pltpu.VMEM, LAYERS + 1),
+        scratch_shapes=[pltpu.VMEM((4096, 128), jnp.float32), pltpu.SemaphoreType.DMA(())],
+        compiler_params=pltpu.CompilerParams(vmem_limit_bytes=20 * MIB),
+        cost_estimate=pl.CostEstimate(flops=0, bytes_accessed=6 * MIB, transcendentals=0),
+        name="pack",
     )(rows, x)
 
 
@@ -331,9 +356,9 @@
     place = jnp.stack([row, col]).astype(jnp.int32)
     rows = jnp.concatenate([below[4:], place, below, at_rows, lies_at])
     head = jnp.concatenate([jnp.zeros(1, jnp.int32), place, jnp.zeros(5, jnp.int32)])
-    first, second, picked, *sends = prepare(jnp.concatenate([head, at_rows, staying, going]), x2)
-    share, packed = sends[:LAYERS], sends[LAYERS:]
-
+    first, second, picked, *share = prepare(jnp.concatenate([head, at_rows, staying]), x2)
+
+    packed = pack(jnp.concatenate([row[None].astype(jnp.int32), jnp.zeros(7, jnp.int32), going]), x2)
     odd = lax.ppermute(packed[LAYERS], "row", [(0, 1)])
     pieces = [jnp.where(row == 0, packed[k], odd[8 * CAP * k : 8 * CAP * (k + 1)]) for k in range(LAYERS)]
     new = jnp.where(row < 2, pieces[0], 0.0)

time: 168 us -> 161 us (0.958)
  waiting for transfers between devices: 79.1 us -> 74.8 us
  local copies, waits for them, and re-layouts: 9.24 us -> 5.91 us
  Pallas kernels: 23.4 us -> 26.3 us
  starting transfers between devices: 29.3 us -> 27.3 us
    unnamed x24 -> x14, local copies, waits for them, and re-layouts: 6.5 us -> 3.1 us
    ppermute x7, waiting for transfers between devices: 33.1 us -> 30.1 us  [few_pivots(): new = new + lax.ppermute(pieces[to], 'row', [(0, 2 * to), (1, 2 * to + 1)])]
    ppermute x7, starting transfers between devices: 7.14 us -> 4.67 us  [few_pivots(): piece = piece + lax.ppermute(share[to], 'row', [(0, 2 * to)])]
    ppermute x1, waiting for transfers between devices: 14.7 us -> 12.7 us  [across(): return value + lax.ppermute(value, 'col', [(i, i + 8) for i in range(8)])]
    pallas_call x0 -> x1, Pallas kernels: none -> 1.75 us  [pack(): pl.pallas_call(pack_kernel, out_shape=[piece] * LAYERS + [group], in_spec...]
    ppermute x1, waiting for transfers between devices: 13.7 us -> 15.4 us  [few_pivots(): lax.ppermute(piece, 'row', [(2 * i, 2 * i + 1) for i in range(LAYERS)])]
  transfers between devices with their start and end apart: 33 -> 33, of which waited for: 7 -> 7; matrix products, arithmetic and copies ran while one was open for 7% -> 8% of each run, Pallas kernels for 4% -> 5%
where the time goes in v3:
time: 161 us; the launch traced here: 160 us
  waiting for transfers between devices  74.8 us (46%)
  starting transfers between devices  27.3 us (17%)
  Pallas kernels  26.3 us (16%)
  between operations  14 us (9%)
  other arithmetic  11.1 us (7%)
  local copies, waits for them, and re-layouts  5.91 us (4%)
    ppermute x7, waiting for transfers between devices, few_pivots(): new = new + lax.ppermute(pieces[to], 'row', [(0, 2 * to), (1, 2 * to + 1)])  30.1 us
    ppermute x1, waiting for transfers between devices, few_pivots(): lax.ppermute(piece, 'row', [(2 * i, 2 * i + 1) for i in range(LAYERS)])  15.4 us
    pallas_call x1, Pallas kernels, trailing(): pl.pallas_call(trailing_kernel, out_shape=jax.ShapeDtypeStruct((8192, 128...  14.2 us
    ppermute x1, waiting for transfers between devices, across(): return value + lax.ppermute(value, 'col', [(i, i + 8) for i in range(8)])  12.7 us
    ppermute x1, waiting for transfers between devices, gather_panel(): mine = mine + lax.ppermute(mine, 'col', [(i, i + 8) for i in range(8)])  8.72 us
    ppermute x4, waiting for transfers between devices, x_shift(): lax.ppermute(value, 'col', [(i, i // 8 * 8 + (i // 2 + by) % 4 * 2 + i %...  7.91 us
    pallas_call x1, Pallas kernels, solve(): pl.pallas_call(solve_kernel, out_shape=[part, part], in_specs=whole(pltpu...  6.1 us
    ppermute x7, starting transfers between devices, few_pivots(): new = new + lax.ppermute(pieces[to], 'row', [(0, 2 * to), (1, 2 * to + 1)])  5.31 us
  transfers between devices with their start and end apart: 33, of which 7 were waited for; matrix products, arithmetic and copies ran while one was open for 8% of the time, Pallas kernels for 5%

profile of v3, /device:TPU:58, one launch (start us, length us, event | category | flops | bytes accessed | tf_op | source)
XLA Modules:
  0.0 160.1 jit_solution(14057787668007876013)
XLA Ops:
  7.2 1.1 convert_reduce_fusion
  9.4 4.2 %prepare.1 = (f32[512,512]{1,0:T(8,128)S(1)}, f32[512,512]{1,0:T(8,128)}, f32[384,128]{1,0:T(8,128)S(1)}, f32[192,128]{1,0:T(8,128)S(1)}, f32[192,128]{1,0:T(8,1...) custom-call(s32[248]{0:T(256)S(1)} %concatenate.24.rows_ref, ...), custom_call_target="tpu_custom_call" | custom-call | bytes 10485760 | tf_op jit(solution)/shard_map/prepare/pallas_call | solution.py:124
  18.3 1.5 collective-permute-start
  19.9 1.3 collective-permute-start.8
  21.2 15.4 %collective-permute-done.8 = f32[192,128]{1,0:T(8,128)S(1)} collective-permute-done((f32[192,128]{1,0:T(8,128)S(1)}, f32[192,128]{1,0:T(8,128)S(1)}, u32[]{:S(2)}, u32[]{:S(2)}) %collective-permute-start.8) | collective-permute-done | bytes 98336 | tf_op jit(solution)/shard_map/ppermute | solution.py:372
  37.5 1.6 %collective-permute-start.9 = (f32[512,512]{1,0:T(8,128)}, f32[512,512]{1,0:T(8,128)}, u32[]{:S(2)}, u32[]{:S(2)}) collective-permute-start(f32[512,512]{1,0:T(8,128)} %get-tuple-element.67), channel_id=1, source_target_pairs={{0,1},{16,17},{32,33},{48,49},{64,65},{80,81},{96,97},{112,113},{1... | collective-permute-start | bytes 3145736 | tf_op jit(solution)/shard_map/ppermute | solution.py:309
  39.4 1.8 %pack.1 = (f32[384,128]{1,0:T(8,128)S(1)}, f32[384,128]{1,0:T(8,128)S(1)}, f32[384,128]{1,0:T(8,128)S(1)}, f32[384,128]{1,0:T(8,128)S(1)}, f32[384,128]{1,0:T(8,...) custom-call(s32[776]{0:T(1024)S(1)} %pad_add_fusion.rows_ref, ...), custom_call_target="tpu_custom_call" | custom-call | bytes 6291456 | tf_op jit(solution)/shard_map/pack/pallas_call | solution.py:156
  41.2 1.9 %collective-permute-start.19 = (f32[3072,128]{1,0:T(8,128)}, f32[3072,128]{1,0:T(8,128)}, u32[]{:S(2)}, u32[]{:S(2)}) collective-permute-start(f32[3072,128]{1,0:T(8,128)} %get-tuple-element.69), channel_id=1, source_target_pairs={{0,16},{1,17},{2,18},{3,19},{4,20},{5,21},{6,22},{7,23},{8,24},{9,... | collective-permute-start | bytes 4718600 | tf_op jit(solution)/shard_map/ppermute | solution.py:362
  46.4 1.0 fusion.29
  47.5 1.3 collective-permute-start.13
  48.8 2.2 %slice_select_fusion.9 = (f32[384,128]{1,0:T(8,128)}, f32[384,128]{1,0:T(8,128)S(1)}, f32[384,128]{1,0:T(8,128)S(1)}, f32[384,128]{1,0:T(8,128)S(1)}, f32[384,12...) fusion(f32[384,128]{1,0:T(8,128)S(1)} %get-tuple-element.70, ...), kind=kLoop, calls=%fused_computation.84 | loop fusion | flops 344064 | bytes 4128769 | tf_op jit(solution)/shard_map/jit(_where)/select_n | solution.py:363
  52.4 1.3 collective-permute-start.25
  54.4 8.7 %collective-permute-done.13 = f32[128,512]{1,0:T(8,128)S(1)} collective-permute-done((f32[128,512]{1,0:T(8,128)S(1)}, f32[128,512]{1,0:T(8,128)S(1)}, u32[]{:S(2)}, u32[]{:S(2)}) %collective-permute-start.13) | collective-permute-done | bytes 262176 | tf_op jit(solution)/shard_map/ppermute | solution.py:319
  65.9 30.1 %collective-permute-done.25 = f32[384,128]{1,0:T(8,128)S(1)} collective-permute-done((f32[384,128]{1,0:T(8,128)S(1)}, f32[384,128]{1,0:T(8,128)S(1)}, u32[]{:S(2)}, u32[]{:S(2)}) %collective-permute-start.25) | collective-permute-done | bytes 196640 | tf_op jit(solution)/shard_map/ppermute | solution.py:366
  96.5 1.5 collective-permute-start.14
  98.0 1.0 fusion.37.new_ref
  99.0 3.6 %collective-permute-done.15 = f32[128,512]{1,0:T(8,128)S(1)} collective-permute-done((f32[128,512]{1,0:T(8,128)S(1)}, f32[128,512]{1,0:T(8,128)S(1)}, u32[]{:S(2)}, u32[]{:S(2)}) %collective-permute-start.15) | collective-permute-done | bytes 262176 | tf_op jit(solution)/shard_map/ppermute | solution.py:295
  103.9 1.0 collective-permute-start.16
  106.3 3.9 %collective-permute-done.16 = f32[64,512]{1,0:T(8,128)S(1)} collective-permute-done((f32[64,512]{1,0:T(8,128)S(1)}, f32[64,512]{1,0:T(8,128)S(1)}, u32[]{:S(2)}, u32[]{:S(2)}) %collective-permute-start.16) | collective-permute-done | bytes 131104 | tf_op jit(solution)/shard_map/ppermute | solution.py:295
  115.4 1.3 concatenate.23.rows_ref
  116.8 1.3 collective-permute-start.31
  118.8 12.7 %collective-permute-done.31 = f32[48,512]{1,0:T(8,128)S(1)} collective-permute-done((f32[48,512]{1,0:T(8,128)S(1)}, f32[48,512]{1,0:T(8,128)S(1)}, u32[]{:S(2)}, u32[]{:S(2)}) %collective-permute-start.31) | collective-permute-done | bytes 98336 | tf_op jit(solution)/shard_map/ppermute | solution.py:330
  132.2 6.1 %solve.1 = (bf16[1024,512]{1,0:T(8,128)(2,1)}, bf16[1024,512]{1,0:T(8,128)(2,1)}) custom-call(s32[568]{0:T(1024)} %concatenate.23.rows_ref, f32[512,512]{1,0:T(8,128)} %constant_dynamic-update-slice_fusion.half_ref, f32[512,512]{1,0:T(8,128)} %collective-permute-done.18.other_ref, f32[48,512]{1,0:T(8,128)} %add.292.sent_ref, f32[512,512]{1,0:T(8,128)S(1)} %copy-done.4), custom_call_target="tpu_custom_call" | custom-call | flops 1610612736 | bytes 6291456 | tf_op jit(solution)/shard_map/solve/pallas_call | solution.py:190
  138.3 14.2 %trailing.1 = f32[8192,128]{1,0:T(8,128)} custom-call(s32[568]{0:T(1024)} %concatenate.23.rows_ref, f32[8192,128]{1,0:T(8,128)} %bitcast.40, f32[7680,128]{1,0:T(8,128)} %all-gather.2.cloned.1.call-done.gathered_all, bf16[1024,512]{1,0:T(8,128)(2,1)} %get-tuple-element.77.l_high_all, bf16[1024,512]{1,0:T(8,128)(2,1)} %get-tuple-element.78.l_low_all, ...), custom_call_target="tpu_custom_call" | custom-call | flops 4831838208 | bytes 18874368 | tf_op jit(solution)/shard_map/trailing/pallas_call | solution.py:274
  (98 shorter events, 26.2 us)
Async XLA Ops:
  6.5 131.8 %all-gather.2.cloned.1.call-start = ((), (), s32[]{:S(2)}) async-start(), calls=%async_computation.2 | async-start | bytes 4423680 | tf_op jit(solution)/shard_map/all_gather | solution.py:304
  14.2 3.4 %collective-permute-start.2 = (f32[192,128]{1,0:T(8,128)S(1)}, f32[192,128]{1,0:T(8,128)S(1)}, u32[]{:S(2)}, u32[]{:S(2)}) collective-permute-start(f32[192,128]{1,0:T(8,128)S(1)} %get-tuple-element.60), channel_id=1, source_target_pairs={{0,96},{1,97},{2,98},{3,99},{4,100},{5,101},{6,102},{7,103},{8,104... | collective-permute-start | bytes 294920 | tf_op jit(solution)/shard_map/ppermute | solution.py:371
  14.9 3.4 %collective-permute-start.3 = (f32[192,128]{1,0:T(8,128)S(1)}, f32[192,128]{1,0:T(8,128)S(1)}, u32[]{:S(2)}, u32[]{:S(2)}) collective-permute-start(f32[192,128]{1,0:T(8,128)S(1)} %get-tuple-element.61), channel_id=1, source_target_pairs={{0,160},{1,161},{2,162},{3,163},{4,164},{5,165},{6,166},{7,167},{8... | collective-permute-start | bytes 294920 | tf_op jit(solution)/shard_map/ppermute | solution.py:371
  15.6 4.2 %collective-permute-start.4 = (f32[192,128]{1,0:T(8,128)S(1)}, f32[192,128]{1,0:T(8,128)S(1)}, u32[]{:S(2)}, u32[]{:S(2)}) collective-permute-start(f32[192,128]{1,0:T(8,128)S(1)} %get-tuple-element.62), channel_id=1, source_target_pairs={{0,64},{1,65},{2,66},{3,67},{4,68},{5,69},{6,70},{7,71},{8,72},{9,... | collective-permute-start | bytes 294920 | tf_op jit(solution)/shard_map/ppermute | solution.py:371
  16.3 3.5 %collective-permute-start.5 = (f32[192,128]{1,0:T(8,128)S(1)}, f32[192,128]{1,0:T(8,128)S(1)}, u32[]{:S(2)}, u32[]{:S(2)}) collective-permute-start(f32[192,128]{1,0:T(8,128)S(1)} %get-tuple-element.63), channel_id=1, source_target_pairs={{0,192},{1,193},{2,194},{3,195},{4,196},{5,197},{6,198},{7,199},{8... | collective-permute-start | bytes 294920 | tf_op jit(solution)/shard_map/ppermute | solution.py:371
  18.3 18.2 %collective-permute-start = (f32[384,128]{1,0:T(8,128)S(1)}, f32[384,128]{1,0:T(8,128)S(1)}, u32[]{:S(2)}, u32[]{:S(2)}) collective-permute-start(f32[384,128]{1,0:T(8,128)S(1)} %get-tuple-element.57), channel_id=1, source_target_pairs={{0,16},{16,0},{32,48},{48,32},{64,80},{80,64},{96,112},{112,96},{1... | collective-permute-start | bytes 589832 | tf_op jit(solution)/shard_map/ppermute | solution.py:299
  19.9 16.7 %collective-permute-start.8 = (f32[192,128]{1,0:T(8,128)S(1)}, f32[192,128]{1,0:T(8,128)S(1)}, u32[]{:S(2)}, u32[]{:S(2)}) collective-permute-start(f32[192,128]{1,0:T(8,128)S(1)} %add_add_fusion.1), channel_id=1, source_target_pairs={{0,16},{32,48},{64,80},{96,112},{128,144},{160,176},{192,208},{224... | collective-permute-start | bytes 294920 | tf_op jit(solution)/shard_map/ppermute | solution.py:372
  37.5 5.6 %collective-permute-start.9 = (f32[512,512]{1,0:T(8,128)}, f32[512,512]{1,0:T(8,128)}, u32[]{:S(2)}, u32[]{:S(2)}) collective-permute-start(f32[512,512]{1,0:T(8,128)} %get-tuple-element.67), channel_id=1, source_target_pairs={{0,1},{16,17},{32,33},{48,49},{64,65},{80,81},{96,97},{112,113},{1... | collective-permute-start | bytes 3145736 | tf_op jit(solution)/shard_map/ppermute | solution.py:309
  41.2 7.6 %collective-permute-start.19 = (f32[3072,128]{1,0:T(8,128)}, f32[3072,128]{1,0:T(8,128)}, u32[]{:S(2)}, u32[]{:S(2)}) collective-permute-start(f32[3072,128]{1,0:T(8,128)} %get-tuple-element.69), channel_id=1, source_target_pairs={{0,16},{1,17},{2,18},{3,19},{4,20},{5,21},{6,22},{7,23},{8,24},{9,... | collective-permute-start | bytes 4718600 | tf_op jit(solution)/shard_map/ppermute | solution.py:362
  47.5 15.6 %collective-permute-start.13 = (f32[128,512]{1,0:T(8,128)S(1)}, f32[128,512]{1,0:T(8,128)S(1)}, u32[]{:S(2)}, u32[]{:S(2)}) collective-permute-start(f32[128,512]{1,0:T(8,128)S(1)} %fusion.29), channel_id=1, source_target_pairs={{0,8},{1,9},{2,10},{3,11},{4,12},{5,13},{6,14},{7,15},{16,24},{17,... | collective-permute-start | bytes 786440 | tf_op jit(solution)/shard_map/ppermute | solution.py:319
  51.0 12.7 %collective-permute-start.20 = (f32[384,128]{1,0:T(8,128)}, f32[384,128]{1,0:T(8,128)S(1)}, u32[]{:S(2)}, u32[]{:S(2)}) collective-permute-start(f32[384,128]{1,0:T(8,128)} %get-tuple-element.103), channel_id=1, source_target_pairs={{0,128},{16,144},{1,129},{17,145},{2,130},{18,146},{3,131},{19,147... | collective-permute-start | bytes 589832 | tf_op jit(solution)/shard_map/ppermute | solution.py:366
  51.7 12.8 %collective-permute-start.26 = (f32[384,128]{1,0:T(8,128)S(1)}, f32[384,128]{1,0:T(8,128)S(1)}, u32[]{:S(2)}, u32[]{:S(2)}) collective-permute-start(f32[384,128]{1,0:T(8,128)S(1)} %get-tuple-element.104), channel_id=1, source_target_pairs={{0,224},{16,240},{1,225},{17,241},{2,226},{18,242},{3,227},{19,243... | collective-permute-start | bytes 589832 | tf_op jit(solution)/shard_map/ppermute | solution.py:366
  52.4 43.6 %collective-permute-start.25 = (f32[384,128]{1,0:T(8,128)S(1)}, f32[384,128]{1,0:T(8,128)S(1)}, u32[]{:S(2)}, u32[]{:S(2)}) collective-permute-start(f32[384,128]{1,0:T(8,128)S(1)} %get-tuple-element.105), channel_id=1, source_target_pairs={{0,32},{16,48},{1,33},{17,49},{2,34},{18,50},{3,35},{19,51},{4,36}... | collective-permute-start | bytes 589832 | tf_op jit(solution)/shard_map/ppermute | solution.py:366
  53.7 42.8 %collective-permute-start.24 = (f32[384,128]{1,0:T(8,128)S(1)}, f32[384,128]{1,0:T(8,128)S(1)}, u32[]{:S(2)}, u32[]{:S(2)}) collective-permute-start(f32[384,128]{1,0:T(8,128)S(1)} %get-tuple-element.106), channel_id=1, source_target_pairs={{0,192},{16,208},{1,193},{17,209},{2,194},{18,210},{3,195},{19,211... | collective-permute-start | bytes 589832 | tf_op jit(solution)/shard_map/ppermute | solution.py:366
  63.1 34.9 %collective-permute-start.23 = (f32[384,128]{1,0:T(8,128)S(1)}, f32[384,128]{1,0:T(8,128)S(1)}, u32[]{:S(2)}, u32[]{:S(2)}) collective-permute-start(f32[384,128]{1,0:T(8,128)S(1)} %get-tuple-element.107), channel_id=1, source_target_pairs={{0,64},{16,80},{1,65},{17,81},{2,66},{18,82},{3,67},{19,83},{4,68}... | collective-permute-start | bytes 589832 | tf_op jit(solution)/shard_map/ppermute | solution.py:366
  63.8 34.2 %collective-permute-start.22 = (f32[384,128]{1,0:T(8,128)S(1)}, f32[384,128]{1,0:T(8,128)S(1)}, u32[]{:S(2)}, u32[]{:S(2)}) collective-permute-start(f32[384,128]{1,0:T(8,128)S(1)} %get-tuple-element.108), channel_id=1, source_target_pairs={{0,160},{16,176},{1,161},{17,177},{2,162},{18,178},{3,163},{19,179... | collective-permute-start | bytes 589832 | tf_op jit(solution)/shard_map/ppermute | solution.py:366
  64.4 33.5 %collective-permute-start.21 = (f32[384,128]{1,0:T(8,128)S(1)}, f32[384,128]{1,0:T(8,128)S(1)}, u32[]{:S(2)}, u32[]{:S(2)}) collective-permute-start(f32[384,128]{1,0:T(8,128)S(1)} %get-tuple-element.109), channel_id=1, source_target_pairs={{0,96},{16,112},{1,97},{17,113},{2,98},{18,114},{3,99},{19,115},{4... | collective-permute-start | bytes 589832 | tf_op jit(solution)/shard_map/ppermute | solution.py:366
  96.0 6.7 %collective-permute-start.15 = (f32[128,512]{1,0:T(8,128)S(1)}, f32[128,512]{1,0:T(8,128)S(1)}, u32[]{:S(2)}, u32[]{:S(2)}) collective-permute-start(f32[128,512]{1,0:T(8,128)S(1)} %get-tuple-element.95), channel_id=1, source_target_pairs={{0,6},{1,7},{2,0},{3,1},{4,2},{5,3},{6,4},{7,5},{8,14},{9,15},{10,... | collective-permute-start | bytes 786440 | tf_op jit(solution)/shard_map/ppermute | solution.py:295
  96.5 7.3 %collective-permute-start.14 = (f32[128,512]{1,0:T(8,128)S(1)}, f32[128,512]{1,0:T(8,128)S(1)}, u32[]{:S(2)}, u32[]{:S(2)}) collective-permute-start(f32[128,512]{1,0:T(8,128)S(1)} %get-tuple-element.95), channel_id=1, source_target_pairs={{0,2},{1,3},{2,4},{3,5},{4,6},{5,7},{6,0},{7,1},{8,10},{9,11},{10,... | collective-permute-start | bytes 786440 | tf_op jit(solution)/shard_map/ppermute | solution.py:295
  102.7 8.2 %collective-permute-start.17 = (f32[64,512]{1,0:T(8,128)S(1)}, f32[64,512]{1,0:T(8,128)S(1)}, u32[]{:S(2)}, u32[]{:S(2)}) collective-permute-start(f32[64,512]{1,0:T(8,128)S(1)} %slice.97), channel_id=1, source_target_pairs={{0,6},{1,7},{2,0},{3,1},{4,2},{5,3},{6,4},{7,5},{8,14},{9,15},{10,... | collective-permute-start | bytes 393224 | tf_op jit(solution)/shard_map/ppermute | solution.py:295
  103.9 6.3 %collective-permute-start.16 = (f32[64,512]{1,0:T(8,128)S(1)}, f32[64,512]{1,0:T(8,128)S(1)}, u32[]{:S(2)}, u32[]{:S(2)}) collective-permute-start(f32[64,512]{1,0:T(8,128)S(1)} %slice.96), channel_id=1, source_target_pairs={{0,2},{1,3},{2,4},{3,5},{4,6},{5,7},{6,0},{7,1},{8,10},{9,11},{10,... | collective-permute-start | bytes 393224 | tf_op jit(solution)/shard_map/ppermute | solution.py:295
  111.5 20.6 %collective-permute-start.18 = (f32[512,512]{1,0:T(8,128)}, f32[512,512]{1,0:T(8,128)}, u32[]{:S(2)}, u32[]{:S(2)}) collective-permute-start(f32[512,512]{1,0:T(8,128)} %constant_dynamic-update-slice_fusion.half_ref), channel_id=1, source_target_pairs={{0,1},{1,0},{2,3},{3,2},{4,5},{5,4},{6,7},{7,6},{8,9},{9,8},{10,11... | collective-permute-start | bytes 3145736 | tf_op jit(solution)/shard_map/ppermute | solution.py:299
  112.7 4.0 %collective-permute-start.30 = (f32[48,512]{1,0:T(8,128)S(1)}, f32[48,512]{1,0:T(8,128)S(1)}, u32[]{:S(2)}, u32[]{:S(2)}) collective-permute-start(f32[48,512]{1,0:T(8,128)S(1)} %fusion.54), channel_id=1, source_target_pairs={{0,4},{1,5},{16,20},{17,21},{32,36},{33,37},{48,52},{49,53},{64,68... | collective-permute-start | bytes 294920 | tf_op jit(solution)/shard_map/ppermute | solution.py:328
  116.8 14.7 %collective-permute-start.31 = (f32[48,512]{1,0:T(8,128)S(1)}, f32[48,512]{1,0:T(8,128)S(1)}, u32[]{:S(2)}, u32[]{:S(2)}) collective-permute-start(f32[48,512]{1,0:T(8,128)S(1)} %add_add_fusion), channel_id=1, source_target_pairs={{0,8},{1,9},{2,10},{3,11},{4,12},{5,13},{6,14},{7,15},{16,24},{17,... | collective-permute-start | bytes 294920 | tf_op jit(solution)/shard_map/ppermute | solution.py:330
  (14 other events, 113.3 us)
Sparse Core Ops, SparseCore 0:
  37.6 52.8 all-gather.1
